TPU v7x, 256 devices: a whole 4x4x8 slice. The times are simulated.
256 devices in a mesh: layer: 4 (over y), grid: 64 (over x, z, core).
Axes of the slice: x: 4, y: 4, z: 8, core: 2. Of those that a mesh axis runs over, the one named last changes fastest.
Arguments:
- density: bfloat16 [512, 128, 1024], P('grid'), may hold values from -0.75 to 0.75
- pattern: int32 [512, 8], replicated, may hold values from 0 to 511, as said below
Outputs:
- purified: float32 [512, 128, 1024], P('grid', None, 'layer')
Inputs may be any that keep to these rules, and one draw needn't show every extreme that they name: `pattern`: row i lists 8 different block columns, i itself among them, each of the form (i + o) mod 512 with -8 <= o <= 8.
All inputs are finite; a program needn't handle non-finite values.
Results may differ from a plain program's by a relative error of at most 0.0029.
Values may be sent and summed in bfloat16 or wider, within the bound.
No kernel may reach another device: no remote copies, remote signals or barrier semaphores. Data moves between devices by JAX's collectives and lax.ppermute only.
A program may use at most 64 MiB of HBM per device.

v0:
```python
import jax
import jax.numpy as jnp
from jax import lax
from jax.sharding import PartitionSpec as P

BAND = 8


def extended(block, sides, width):
    for axis, dim in sides:
        count = lax.axis_size(axis)
        forward = [(i, i + 1) for i in range(count - 1)]
        forward.append((count - 1, 0))
        backward = [(target, source) for source, target in forward]
        low = lax.ppermute(
            lax.slice_in_dim(block, block.shape[dim] - width, None, axis=dim), axis, forward
        )
        high = lax.ppermute(lax.slice_in_dim(block, 0, width, axis=dim), axis, backward)
        block = jnp.concatenate([low, block, high], axis=dim)
    return block


def local(density, pattern):
    rows_dev, block_size, span_cols = density.shape
    listed = pattern.shape[1]
    blocks = pattern.shape[0]
    layer_count = lax.axis_size("layer")
    slot_share = listed // layer_count
    grid_index = lax.axis_index("grid")
    layer_index = lax.axis_index("layer")
    first_row = grid_index * rows_dev
    slot_start = layer_index * slot_share
    own_pattern = lax.dynamic_slice_in_dim(pattern, first_row, rows_dev, 0)
    padded = extended(density, (("grid", 0),), BAND)
    padded_blocks = padded.reshape(padded.shape[0], block_size, listed, block_size)
    slot_cols = lax.dynamic_slice_in_dim(own_pattern, slot_start, slot_share, 1)
    neighbours = jnp.take(pattern, slot_cols, axis=0)
    selector = (neighbours[:, :, :, None] == own_pattern[:, None, None, :]).astype(jnp.bfloat16)
    located = (slot_cols - first_row + BAND) % blocks

    def align_row(row_items):
        row_places, choosing = row_items
        fetched = jnp.take(padded_blocks, row_places, axis=0)
        return jnp.einsum(
            "abj,aybz->ayjz", choosing, fetched, preferred_element_type=jnp.float32
        ).astype(jnp.bfloat16)

    aligned = lax.map(align_row, (located, selector))
    left_slots = lax.dynamic_slice_in_dim(
        density.reshape(rows_dev, block_size, listed, block_size), slot_start, slot_share, 2
    )
    partial_value = jnp.einsum(
        "ixay,iayjz->ixjz", left_slots, aligned, preferred_element_type=jnp.float32
    )
    square_part = lax.psum_scatter(partial_value, "layer", scatter_dimension=2, tiled=True)
    square = square_part.astype(jnp.bfloat16)
    cube_terms = jnp.einsum("ixay,iayjz->ixjz", square, aligned, preferred_element_type=jnp.float32)
    cube_part = lax.psum_scatter(cube_terms, "layer", scatter_dimension=2, tiled=True)
    result = 3.0 * square.astype(jnp.float32) - 2.0 * cube_part
    return result.reshape(rows_dev, block_size, slot_share * block_size)


def solution(mesh):
    placed = (P("grid", None, None), P())
    return jax.shard_map(
        local, mesh=mesh, in_specs=placed, out_specs=P("grid", None, "layer"), check_vma=False
    )
```

profile of v0, /device:TPU:16, one launch (start us, length us, event | category | flops | bytes accessed | tf_op | source)
XLA Modules:
  0.0 276.7 jit_solution(17797892067483419186)
XLA Ops:
  6.6 7.6 %collective-permute-start.1 = (bf16[8,128,1024]{2,1,0:T(8,128)(2,1)}, bf16[8,128,1024]{2,1,0:T(8,128)(2,1)}, u32[]{:S(2)}, u32[]{:S(2)}) collective-permute-start(bf16[8,128,1024]{2,1,0:T(8,128)(2,1)} %param.4), channel_id=1, source_target_pairs={{1,0},{2,1},{3,2},{4,3},{5,4},{6,5},{7,6},{8,7},{9,8},{10,9},{11,1... | collective-permute-start | bytes 6291464 | tf_op jit(solution)/shard_map/ppermute | solution.py:18
  14.2 3.9 %copy.20 = bf16[8,128,1024]{1,2,0:T(8,128)(2,1)} copy(bf16[8,128,1024]{2,1,0:T(8,128)(2,1)} %param.4) | data formatting | bytes 4194304 | tf_op args[0]
  18.4 0.6 gather_fusion.1
  19.2 0.6 dynamic-slice
  20.8 17.4 %collective-permute-done = bf16[8,128,1024]{2,1,0:T(8,128)(2,1)} collective-permute-done((bf16[8,128,1024]{2,1,0:T(8,128)(2,1)}, bf16[8,128,1024]{2,1,0:T(8,128)(2,1)}, u32[]{:S(2)}, u32[]{:S(2)}) %collective-permute-start) | collective-permute-done | bytes 2097184 | tf_op jit(solution)/shard_map/ppermute | solution.py:15
  38.2 3.2 %pad_maximum_fusion = bf16[24,128,1024]{2,1,0:T(8,128)(2,1)S(1)} fusion(bf16[8,128,1024]{2,1,0:T(8,128)(2,1)} %collective-permute-done.1, bf16[8,128,1024]{2,1,0:T(8,128)(2,1)S(1)} %copy-done, bf16[8,128,1024]{2,1,0:T(8,128)(2,1)} %collective-permute-done), kind=kLoop, calls=%fused_computation.18 | loop fusion | flops 6291456 | bytes 12582912 | tf_op jit(solution)/shard_map/concatenate | solution.py:19
  41.3 4.3 %copy.47 = bf16[384,8,8,128]{3,2,1,0:T(8,128)(2,1)} copy(bf16[384,8,8,128]{3,1,2,0:T(8,128)(2,1)S(1)} %bitcast.70) | data formatting | bytes 12582912
  45.6 38.1 %while.10 = (s32[]{:T(128)}, bf16[8,2,128,8,128]{4,2,1,3,0:T(8,128)(2,1)}, s32[8,2]{1,0:T(8,128)S(1)}, bf16[24,128,8,128]{3,2,1,0:T(8,128)(2,1)}, bf16[8,2,8,8]{3,2,1,0:T(8,128)(2,1)S(1)}, /*index=5*/s32[]{:T(128)}) while((s32[]{:T(128)}, bf16[8,2,128,8,128]{4,2,1,3,0:T(8,128)(2,1)}, s32[8,2]{1,0:T(8,128)S(1)}, ...), condition=%wide.region_1.2_spmd, body=%wide.region_0.1_spmd.sunk | while | flops 4719636 | bytes 3155067 | solution.py:48
  45.6 3.4 %gather_fusion = bf16[2,128,8,128]{3,2,1,0:T(8,128)(2,1)S(1)} fusion(bf16[24,128,8,128]{3,2,1,0:T(8,128)(2,1)} %get-tuple-element.91, s32[1024]{0:T(1024)S(1)} %pad_clamp_fusion.3), kind=kCustom, calls=%fused_computation.clone.1 | custom fusion | bytes 1048584 | tf_op jit(solution)/shard_map/while/body/eval_jaxpr/jit(_take)/gather | solution.py:43
  49.1 0.4 fusion.24
  49.5 0.9 copy_dynamic-update-slice_fusion.2
  50.4 3.4 %gather_fusion = bf16[2,128,8,128]{3,2,1,0:T(8,128)(2,1)S(1)} fusion(bf16[24,128,8,128]{3,2,1,0:T(8,128)(2,1)} %get-tuple-element.91, s32[1024]{0:T(1024)S(1)} %pad_clamp_fusion.3), kind=kCustom, calls=%fused_computation.clone.1 | custom fusion | bytes 1048584 | tf_op jit(solution)/shard_map/while/body/eval_jaxpr/jit(_take)/gather | solution.py:43
  54.2 0.9 copy_dynamic-update-slice_fusion.2
  55.2 3.4 %gather_fusion = bf16[2,128,8,128]{3,2,1,0:T(8,128)(2,1)S(1)} fusion(bf16[24,128,8,128]{3,2,1,0:T(8,128)(2,1)} %get-tuple-element.91, s32[1024]{0:T(1024)S(1)} %pad_clamp_fusion.3), kind=kCustom, calls=%fused_computation.clone.1 | custom fusion | bytes 1048584 | tf_op jit(solution)/shard_map/while/body/eval_jaxpr/jit(_take)/gather | solution.py:43
  59.0 0.9 copy_dynamic-update-slice_fusion.2
  59.9 3.4 %gather_fusion = bf16[2,128,8,128]{3,2,1,0:T(8,128)(2,1)S(1)} fusion(bf16[24,128,8,128]{3,2,1,0:T(8,128)(2,1)} %get-tuple-element.91, s32[1024]{0:T(1024)S(1)} %pad_clamp_fusion.3), kind=kCustom, calls=%fused_computation.clone.1 | custom fusion | bytes 1048584 | tf_op jit(solution)/shard_map/while/body/eval_jaxpr/jit(_take)/gather | solution.py:43
  63.7 0.9 copy_dynamic-update-slice_fusion.2
  64.7 3.4 %gather_fusion = bf16[2,128,8,128]{3,2,1,0:T(8,128)(2,1)S(1)} fusion(bf16[24,128,8,128]{3,2,1,0:T(8,128)(2,1)} %get-tuple-element.91, s32[1024]{0:T(1024)S(1)} %pad_clamp_fusion.3), kind=kCustom, calls=%fused_computation.clone.1 | custom fusion | bytes 1048584 | tf_op jit(solution)/shard_map/while/body/eval_jaxpr/jit(_take)/gather | solution.py:43
  68.1 0.4 fusion.24
  68.5 1.0 copy_dynamic-update-slice_fusion.2
  69.5 3.4 %gather_fusion = bf16[2,128,8,128]{3,2,1,0:T(8,128)(2,1)S(1)} fusion(bf16[24,128,8,128]{3,2,1,0:T(8,128)(2,1)} %get-tuple-element.91, s32[1024]{0:T(1024)S(1)} %pad_clamp_fusion.3), kind=kCustom, calls=%fused_computation.clone.1 | custom fusion | bytes 1048584 | tf_op jit(solution)/shard_map/while/body/eval_jaxpr/jit(_take)/gather | solution.py:43
  73.3 0.9 copy_dynamic-update-slice_fusion.2
  74.3 3.4 %gather_fusion = bf16[2,128,8,128]{3,2,1,0:T(8,128)(2,1)S(1)} fusion(bf16[24,128,8,128]{3,2,1,0:T(8,128)(2,1)} %get-tuple-element.91, s32[1024]{0:T(1024)S(1)} %pad_clamp_fusion.3), kind=kCustom, calls=%fused_computation.clone.1 | custom fusion | bytes 1048584 | tf_op jit(solution)/shard_map/while/body/eval_jaxpr/jit(_take)/gather | solution.py:43
  78.1 0.9 copy_dynamic-update-slice_fusion.2
  79.0 3.4 %gather_fusion = bf16[2,128,8,128]{3,2,1,0:T(8,128)(2,1)S(1)} fusion(bf16[24,128,8,128]{3,2,1,0:T(8,128)(2,1)} %get-tuple-element.91, s32[1024]{0:T(1024)S(1)} %pad_clamp_fusion.3), kind=kCustom, calls=%fused_computation.clone.1 | custom fusion | bytes 1048584 | tf_op jit(solution)/shard_map/while/body/eval_jaxpr/jit(_take)/gather | solution.py:43
  82.9 0.9 copy_dynamic-update-slice_fusion.2
  83.7 5.1 %convolution_bitcast_fusion.1 = f32[8,128,8,128]{3,1,2,0:T(8,128)} fusion(bf16[8,2,128,8,128]{4,2,1,3,0:T(8,128)(2,1)} %get-tuple-element.32, bf16[8,128,8,128]{1,3,2,0:T(8,128)(2,1)} %bitcast.73, s32[]{:T(128)S(6)} %select_n.51), kind=kOutput, calls=%fused_computation.20 | convolution fusion | flops 536870912 | bytes 8912900 | tf_op jit(solution)/shard_map/ixay,iayjz->ixjz/dot_general | solution.py:52
  88.8 71.5 %all-reduce.6 = bf16[8,128,8,128]{3,1,2,0:T(8,128)(2,1)S(1)} all-reduce(f32[8,128,8,128]{3,1,2,0:T(8,128)} %convolution_bitcast_fusion.1), channel_id=2, replica_groups=mesh['layer'=4,'grid'=64] {'layer'}, use_global_device_ids=true, to_apply=%region_2.3.clone | all-reduce | flops 1048576 | bytes 6291456
  160.7 4.9 %convolution_bitcast_fusion = f32[8,128,8,128]{3,1,2,0:T(8,128)} fusion(bf16[8,2,128,8,128]{4,2,1,3,0:T(8,128)(2,1)} %get-tuple-element.32, bf16[8,128,2,128]{1,3,2,0:T(8,128)(2,1)S(1)} %copy.26), kind=kOutput, calls=%fused_computation.19 | convolution fusion | flops 536870912 | bytes 8912896 | tf_op jit(solution)/shard_map/ixay,iayjz->ixjz/dot_general | solution.py:57
  165.6 101.2 %all-reduce.5.cloned.1.call-done = f32[8,128,8,128]{3,1,2,0:T(8,128)} async-done(((f32[8,128,8,128]{3,1,2,0:T(8,128)}), f32[8,128,8,128]{3,1,2,0:T(8,128)}) %all-reduce.5.cloned.1.call-update) | async-done | bytes 4194320
  266.8 1.3 constant_dynamic-slice_fusion.1
  268.6 1.3 copy.30
  (54 shorter events, 4.1 us)
Async XLA Ops:
  6.5 12.6 %copy-start.2 = (u32[256]{0:T(256)S(1)}, u32[256]{0:T(256)}, u32[]{:S(2)}) copy-start(u32[256]{0:T(256)} %constant.90) | copy-start | bytes 3076
  6.5 31.6 %copy-start = (bf16[8,128,1024]{2,1,0:T(8,128)(2,1)S(1)}, bf16[8,128,1024]{2,1,0:T(8,128)(2,1)}, u32[]{:S(2)}) copy-start(bf16[8,128,1024]{2,1,0:T(8,128)(2,1)} %param.4) | copy-start | bytes 6291460
  6.5 11.6 %copy-start.1 = (s32[512,8]{0,1:T(8,128)S(1)}, s32[512,8]{0,1:T(8,128)}, u32[]{:S(2)}) copy-start(s32[512,8]{0,1:T(8,128)} %param.5) | copy-start | bytes 49156
  6.5 260.3 %all-reduce.5.cloned.1.call-start = ((), (), s32[]{:S(2)}) async-start(), calls=%async_computation | async-start | bytes 8388608
  6.5 31.6 %collective-permute-start = (bf16[8,128,1024]{2,1,0:T(8,128)(2,1)}, bf16[8,128,1024]{2,1,0:T(8,128)(2,1)}, u32[]{:S(2)}, u32[]{:S(2)}) collective-permute-start(bf16[8,128,1024]{2,1,0:T(8,128)(2,1)} %param.4), channel_id=1, source_target_pairs={{0,1},{1,2},{2,3},{3,4},{4,5},{5,6},{6,7},{7,8},{8,9},{9,10},{10,1... | collective-permute-start | bytes 6291464 | tf_op jit(solution)/shard_map/ppermute | solution.py:15
  6.6 31.5 %collective-permute-start.1 = (bf16[8,128,1024]{2,1,0:T(8,128)(2,1)}, bf16[8,128,1024]{2,1,0:T(8,128)(2,1)}, u32[]{:S(2)}, u32[]{:S(2)}) collective-permute-start(bf16[8,128,1024]{2,1,0:T(8,128)(2,1)} %param.4), channel_id=1, source_target_pairs={{1,0},{2,1},{3,2},{4,3},{5,4},{6,5},{7,6},{8,7},{9,8},{10,9},{11,1... | collective-permute-start | bytes 6291464 | tf_op jit(solution)/shard_map/ppermute | solution.py:18
Sparse Core Ops, SparseCore 0:
  165.8 100.9 all-reduce.4
where the time goes:
time: 280 us; the launch traced here: 277 us
  waiting for transfers between devices  119 us (42%)
  blocking collectives  71.5 us (26%)
  local copies, waits for them, and re-layouts  47.8 us (17%)
  between operations  14.2 us (5%)
  matrix products  12.9 us (5%)
  starting transfers between devices  7.65 us (3%)
  other arithmetic  3.91 us (1%)
    unnamed x2, waiting for transfers between devices  101 us
    unnamed x1, blocking collectives  71.5 us
    gather x8, local copies, waits for them, and re-layouts, align_row(): fetched = jnp.take(padded_blocks, row_places, axis=0)  27.4 us
    ppermute x1, waiting for transfers between devices, extended(): lax.ppermute(lax.slice_in_dim(block, block.shape[dim] - width, None, axis...  17.4 us
    unnamed x12, local copies, waits for them, and re-layouts  10.3 us
    ppermute x1, starting transfers between devices, extended(): lax.ppermute(lax.slice_in_dim(block, 0, width, axis=dim), axis, backward)  7.57 us
    dynamic_update_slice x8, local copies, waits for them, and re-layouts, local(): aligned = lax.map(align_row, (located, selector))  7.35 us
  transfers between devices with their start and end apart: 3, of which 2 were waited for; matrix products, arithmetic and copies ran while one was open for 2% of the time, Pallas kernels for 0%

commit v1 on v0

v1 whole, which is shorter than its diff:
```python
import jax
import jax.numpy as jnp
from jax import lax
from jax.experimental import pallas as pl
from jax.experimental.pallas import tpu as pltpu
from jax.sharding import PartitionSpec as P

ROWS = 8
LISTED = 8
BS = 128
ZERO = 3 * ROWS * LISTED


def locate(pattern, grid_index):
    blocks = pattern.shape[0]
    first = grid_index * ROWS
    ring = jnp.concatenate([pattern[-ROWS:], pattern, pattern[:ROWS]], axis=0)
    window = lax.dynamic_slice_in_dim(ring, first, 3 * ROWS, 0)
    rel = (window - first + ROWS) % blocks
    rel = jnp.where(rel >= blocks // 2, rel - blocks, rel)
    own = rel[ROWS : 2 * ROWS]
    chosen = own[:, :, None] == jnp.arange(3 * ROWS, dtype=jnp.int32)
    listed = jnp.sum(jnp.where(chosen[..., None], rel[None, None], 0), axis=2)
    same = listed[:, :, None, :] == own[:, None, :, None]
    slot = jnp.sum(jnp.where(same, jnp.arange(LISTED, dtype=jnp.int32), 0), axis=3)
    place = own[:, :, None] * LISTED + slot
    return jnp.where(jnp.any(same, axis=3), place, ZERO).reshape(-1)


def kernel(meta, loc, own, inner, near, swapped, far, out, buf, square, result, sems, out_sems):
    parity, layer = meta[0], meta[1]
    half = lax.rem(layer, 2)
    outer_base = 16 * parity
    inner_base = 16 - outer_base
    sender = 1 - parity

    copies = [
        pltpu.make_async_copy(own, buf.at[pl.ds(ROWS, ROWS)], sems.at[0]),
        pltpu.make_async_copy(inner, buf.at[pl.ds(inner_base, ROWS)], sems.at[1]),
        pltpu.make_async_copy(near, buf.at[pl.ds(outer_base + 4 * sender + 2 * half, 2)], sems.at[2]),
        pltpu.make_async_copy(
            swapped, buf.at[pl.ds(outer_base + 4 * sender + 2 * (1 - half), 2)], sems.at[3]
        ),
        pltpu.make_async_copy(far, buf.at[pl.ds(outer_base + 4 * parity, 4)], sems.at[4]),
    ]
    for copy in copies:
        copy.start()
    buf[3 * ROWS, :, :BS] = jnp.zeros((BS, BS), jnp.bfloat16)
    for copy in copies:
        copy.wait()

    def block(i, c, a):
        place = loc[i * (LISTED * LISTED) + c * LISTED + a]
        start = pl.multiple_of(lax.rem(place, LISTED) * BS, BS)
        return buf[lax.div(place, LISTED), :, pl.ds(start, BS)]

    def tile(i, c, a):
        return jnp.concatenate(
            [
                jnp.concatenate([block(i, c, a), block(i, c, a + 1)], axis=1),
                jnp.concatenate([block(i, c + 1, a), block(i, c + 1, a + 1)], axis=1),
            ],
            axis=0,
        )

    def times(left, i, a):
        total = jnp.zeros((BS, 2 * BS), jnp.float32)
        for c in range(0, LISTED, 2):
            total += jnp.dot(
                left(c), tile(i, c, a), preferred_element_type=jnp.float32
            )
        return total

    def one_row(i, carry):
        for a in range(0, LISTED, 2):
            part = times(lambda c: buf[ROWS + i, :, c * BS : (c + 2) * BS], i, a)
            square[:, a * BS : (a + 2) * BS] = part.astype(jnp.bfloat16)
        cube = times(lambda c: square[:, c * BS : (c + 2) * BS], i, 2 * layer)
        start = pl.multiple_of(layer * 2 * BS, 2 * BS)
        result[i] = 3.0 * square[:, pl.ds(start, 2 * BS)].astype(jnp.float32) - 2.0 * cube
        pltpu.make_async_copy(result.at[i], out.at[i], out_sems.at[i]).start()
        return carry

    lax.fori_loop(0, ROWS, one_row, 0)
    for i in range(ROWS):
        pltpu.make_async_copy(result.at[i], out.at[i], out_sems.at[i]).wait()


def local(density, pattern):
    grid = lax.axis_size("grid")
    layers = lax.axis_size("layer")
    g = lax.axis_index("grid")
    layer = lax.axis_index("layer")
    parity = g % 2
    half = layer % 2
    outer_pairs = [(i, (i - 1) % grid if i % 2 == 0 else (i + 1) % grid) for i in range(grid)]
    inner_pairs = [(i, i + 1 if i % 2 == 0 else i - 1) for i in range(grid)]
    swap_pairs = []
    for y in range(layers):
        for i in range(grid):
            other = (y ^ 1) if i % 2 == 0 else ((y + 1) ^ 1) - 1
            swap_pairs.append((y * grid + i, (other % layers) * grid + i))
    near_send = lax.dynamic_slice_in_dim(density, 4 * parity + 2 * half, 2, 0)
    near = lax.ppermute(near_send, "grid", outer_pairs)
    far_send = lax.dynamic_slice_in_dim(density, 4 * (1 - parity), 4, 0)
    far = lax.ppermute(far_send, "grid", outer_pairs)
    inner = lax.ppermute(density, "grid", inner_pairs)
    swapped = lax.ppermute(near, ("layer", "grid"), swap_pairs)
    loc = locate(pattern, g)
    meta = jnp.stack([parity, layer]).astype(jnp.int32)
    any_space = pl.BlockSpec(memory_space=pl.ANY)
    smem = pl.BlockSpec(memory_space=pltpu.SMEM)
    return pl.pallas_call(
        kernel,
        out_shape=jax.ShapeDtypeStruct((ROWS, BS, 2 * BS), jnp.float32),
        in_specs=[smem, smem] + [any_space] * 5,
        out_specs=any_space,
        scratch_shapes=[
            pltpu.VMEM((3 * ROWS + 1, BS, LISTED * BS), jnp.bfloat16),
            pltpu.VMEM((BS, LISTED * BS), jnp.bfloat16),
            pltpu.VMEM((ROWS, BS, 2 * BS), jnp.float32),
            pltpu.SemaphoreType.DMA((5,)),
            pltpu.SemaphoreType.DMA((ROWS,)),
        ],
        compiler_params=pltpu.CompilerParams(vmem_limit_bytes=16 * 1024 * 1024),
        cost_estimate=pl.CostEstimate(flops=2_700_000_000, bytes_accessed=8_000_000, transcendentals=0),
    )(meta, loc, density, inner, near, swapped, far)


def solution(mesh):
    placed = (P("grid", None, None), P())
    return jax.shard_map(
        local, mesh=mesh, in_specs=placed, out_specs=P("grid", None, "layer"), check_vma=False
    )
```

time: 280 us -> 41.5 us (0.15); the launches traced: 277 us -> 41.4 us
  waiting for transfers between devices: 119 us -> 12.1 us
  blocking collectives: 71.5 us -> 0 us
  local copies, waits for them, and re-layouts: 47.8 us -> 4.61 us
  between operations: 14.2 us -> 0.06 us
  matrix products: 12.9 us -> 0 us
  Pallas kernels: 0 us -> 11.3 us
    unnamed x2 -> x0, waiting for transfers between devices: 101 us -> none
    unnamed x1 -> x0, blocking collectives: 71.5 us -> none
    gather x9 -> x0, local copies, waits for them, and re-layouts: 28 us -> none  [the longest x8 27.4 us: align_row(): fetched = jnp.take(padded_blocks, row_places, axis=0)]
    dot_general x10 -> x0, matrix products: 12.9 us -> none  [the longest x1 5.07 us: local(): jnp.einsum('ixay,iayjz->ixjz', left_slots, aligned, preferred_element_typ...]
    pallas_call x0 -> x1, Pallas kernels: none -> 11.3 us  [local(): pl.pallas_call(kernel, out_shape=jax.ShapeDtypeStruct((ROWS, BS, 2 * BS),...]
    unnamed x12 -> x4, local copies, waits for them, and re-layouts: 10.3 us -> 0.01 us
    dynamic_update_slice x8 -> x0, local copies, waits for them, and re-layouts: 7.35 us -> none  [local(): aligned = lax.map(align_row, (located, selector))]
    ppermute x2 -> x4, waiting for transfers between devices: 17.4 us -> 12.1 us  [the longest x1 5.49 us: local(): swapped = lax.ppermute(near, ('layer', 'grid'), swap_pairs)]
  transfers between devices with their start and end apart: 3 -> 4, of which waited for: 2 -> 3; matrix products, arithmetic and copies ran while one was open for 2% -> 21% of each run, Pallas kernels for 0% -> 0%
where the time goes in v1:
time: 41.5 us; the launch traced here: 41.4 us
  waiting for transfers between devices  12.1 us (29%)
  Pallas kernels  11.3 us (27%)
  starting transfers between devices  9.27 us (22%)
  local copies, waits for them, and re-layouts  4.61 us (11%)
  other arithmetic  4.02 us (10%)
    pallas_call x1, Pallas kernels, local(): pl.pallas_call(kernel, out_shape=jax.ShapeDtypeStruct((ROWS, BS, 2 * BS),...  11.3 us
    ppermute x1, starting transfers between devices, local(): near = lax.ppermute(near_send, 'grid', outer_pairs)  7.98 us
    ppermute x1, waiting for transfers between devices, local(): swapped = lax.ppermute(near, ('layer', 'grid'), swap_pairs)  5.49 us
    ppermute x1, waiting for transfers between devices, local(): far = lax.ppermute(far_send, 'grid', outer_pairs)  3.34 us
    ppermute x1, waiting for transfers between devices, local(): near = lax.ppermute(near_send, 'grid', outer_pairs)  3.28 us
    dynamic_slice x1, local copies, waits for them, and re-layouts, local(): far_send = lax.dynamic_slice_in_dim(density, 4 * (1 - parity), 4, 0)  2.26 us
    dynamic_slice x1, local copies, waits for them, and re-layouts, local(): near_send = lax.dynamic_slice_in_dim(density, 4 * parity + 2 * half, 2, 0)  2.03 us
    ppermute x1, starting transfers between devices, local(): swapped = lax.ppermute(near, ('layer', 'grid'), swap_pairs)  1.28 us
  transfers between devices with their start and end apart: 4, of which 3 were waited for; matrix products, arithmetic and copies ran while one was open for 21% of the time, Pallas kernels for 0%

profile of v1, /device:TPU:16, one launch (start us, length us, event | category | flops | bytes accessed | tf_op | source)
XLA Modules:
  0.0 41.4 jit_solution(7880951377220186288)
XLA Ops:
  0.0 0.0 copy-start
  0.0 0.0 copy-start.1
  0.0 0.0 collective-permute-start
  0.0 2.0 %constant_dynamic-slice_fusion = bf16[2,128,1024]{2,1,0:T(8,128)(2,1)} fusion(bf16[8,128,1024]{2,1,0:T(8,128)(2,1)} %own.1, s32[]{:T(128)S(6)} %select_n.55), kind=kLoop, calls=%fused_computation.19 | loop fusion | bytes 1048580 | tf_op jit(solution)/shard_map/dynamic_slice | solution.py:103
  2.1 8.0 %collective-permute-start.1 = (bf16[2,128,1024]{2,1,0:T(8,128)(2,1)}, bf16[2,128,1024]{2,1,0:T(8,128)(2,1)}, u32[]{:S(2)}, u32[]{:S(2)}) collective-permute-start(bf16[2,128,1024]{2,1,0:T(8,128)(2,1)} %constant_dynamic-slice_fusion), channel_id=1, source_target_pairs={{0,63},{1,2},{2,1},{3,4},{4,3},{5,6},{6,5},{7,8},{8,7},{9,10},{10,... | collective-permute-start | bytes 1572872 | tf_op jit(solution)/shard_map/ppermute | solution.py:104
  10.1 2.3 %constant_dynamic-slice_fusion.1 = bf16[4,128,1024]{2,1,0:T(8,128)(2,1)} fusion(bf16[8,128,1024]{2,1,0:T(8,128)(2,1)} %own.1, s32[]{:T(128)S(6)} %select_n.56), kind=kLoop, calls=%fused_computation.20 | loop fusion | bytes 2097156 | tf_op jit(solution)/shard_map/dynamic_slice | solution.py:105
  12.3 0.0 collective-permute-start.3
  12.3 0.0 copy-done.1
  12.3 0.1 fusion.6
  12.4 0.1 compare_select_fusion.1
  12.5 0.1 broadcast_multiply_fusion
  12.6 0.1 copy.9
  12.6 0.1 copy.7
  12.7 0.1 iota_compare_fusion
  12.8 1.2 %select_reduce_fusion = s32[8,8,8]{2,1,0:T(8,128)S(1)} fusion(s32[24,8]{0,1:T(8,128)S(1)} %compare_select_fusion.1, pred[8,8,24]{2,1,0:T(8,128)(4,1)S(1)} %iota_compare_fusion), kind=kLoop, calls=%fused_computation.3 | loop fusion | flops 24064 | bytes 4352 | tf_op jit(solution)/shard_map/reduce_sum | solution.py:23
  14.0 3.3 %collective-permute-done.1.near = bf16[2,128,1024]{2,1,0:T(8,128)(2,1)} collective-permute-done((bf16[2,128,1024]{2,1,0:T(8,128)(2,1)}, bf16[2,128,1024]{2,1,0:T(8,128)(2,1)}, u32[]{:S(2)}, u32[]{:S(2)}) %collective-permute-start.1) | collective-permute-done | bytes 524320 | tf_op jit(solution)/shard_map/ppermute | solution.py:104
  17.2 1.3 %collective-permute-start.2 = (bf16[2,128,1024]{2,1,0:T(8,128)(2,1)}, bf16[2,128,1024]{2,1,0:T(8,128)(2,1)}, u32[]{:S(2)}, u32[]{:S(2)}) collective-permute-start(bf16[2,128,1024]{2,1,0:T(8,128)(2,1)} %collective-permute-done.1.near), channel_id=1, source_target_pairs={{0,64},{1,193},{2,66},{3,195},{4,68},{5,197},{6,70},{7,199},{8,72}... | collective-permute-start | bytes 1572872 | tf_op jit(solution)/shard_map/ppermute | solution.py:108
  18.5 1.2 %compare_reduce_fusion = pred[8,8,8]{2,1,0:T(8,128)(4,1)S(1)} fusion(s32[8,8]{1,0:T(8,128)S(1)} %copy.7, s32[8,8,8]{2,1,0:T(8,128)S(1)} %select_reduce_fusion), kind=kLoop, calls=%fused_computation.1 | loop fusion | flops 7680 | bytes 2816 | tf_op jit(solution)/shard_map/reduce_or | solution.py:27
  19.8 1.2 %fusion = s32[8,8,8]{2,1,0:T(8,128)S(1)} fusion(s32[8,8]{1,0:T(8,128)S(1)} %copy.7, s32[8,8,8]{2,1,0:T(8,128)S(1)} %select_reduce_fusion), kind=kLoop, calls=%fused_computation.2 | loop fusion | flops 11776 | bytes 4352 | tf_op jit(solution)/shard_map/reduce_sum | solution.py:25
  21.0 0.1 add_select_fusion
  21.1 0.1 select_n.53.loc
  21.2 0.1 pad_add_fusion.meta
  21.2 5.5 %collective-permute-done.2.swapped = bf16[2,128,1024]{2,1,0:T(8,128)(2,1)} collective-permute-done((bf16[2,128,1024]{2,1,0:T(8,128)(2,1)}, bf16[2,128,1024]{2,1,0:T(8,128)(2,1)}, u32[]{:S(2)}, u32[]{:S(2)}) %collective-permute-start.2) | collective-permute-done | bytes 524320 | tf_op jit(solution)/shard_map/ppermute | solution.py:108
  26.7 3.3 %collective-permute-done.3.far = bf16[4,128,1024]{2,1,0:T(8,128)(2,1)S(1)} collective-permute-done((bf16[4,128,1024]{2,1,0:T(8,128)(2,1)}, bf16[4,128,1024]{2,1,0:T(8,128)(2,1)S(1)}, u32[]{:S(2)}, u32[]{:S(2)}) %collective-permute-start.3) | collective-permute-done | bytes 1048608 | tf_op jit(solution)/shard_map/ppermute | solution.py:106
  30.1 0.0 collective-permute-done.inner
  30.1 0.0 copy-done
  30.1 11.3 %shard_map.28 = f32[8,128,256]{2,1,0:T(8,128)} custom-call(s32[2]{0:T(128)S(1)} %pad_add_fusion.meta, s32[512]{0:T(512)S(1)} %select_n.53.loc, bf16[8,128,1024]{2,1,0:T(8,128)(2,1)S(1)} %copy-done, bf16[8,128,1024]{2,1,0:T(8,128)(2,1)} %collective-permute-done.inner, bf16[2,128,1024]{2,1,0:T(8,128)(2,1)} %collective-permute-done.1.near, ...), custom_call_target="tpu_custom_call" | custom-call | flops 2700000000 | bytes 8000000 | tf_op jit(solution)/shard_map/pallas_call | solution.py:113
Async XLA Ops:
  0.0 30.1 %copy-start = (bf16[8,128,1024]{2,1,0:T(8,128)(2,1)S(1)}, bf16[8,128,1024]{2,1,0:T(8,128)(2,1)}, u32[]{:S(2)}) copy-start(bf16[8,128,1024]{2,1,0:T(8,128)(2,1)} %own.1) | copy-start | bytes 6291460
  0.0 12.3 %copy-start.1 = (s32[512,8]{0,1:T(8,128)S(1)}, s32[512,8]{0,1:T(8,128)}, u32[]{:S(2)}) copy-start(s32[512,8]{0,1:T(8,128)} %param.3) | copy-start | bytes 49156
  0.0 30.1 %collective-permute-start = (bf16[8,128,1024]{2,1,0:T(8,128)(2,1)}, bf16[8,128,1024]{2,1,0:T(8,128)(2,1)}, u32[]{:S(2)}, u32[]{:S(2)}) collective-permute-start(bf16[8,128,1024]{2,1,0:T(8,128)(2,1)} %own.1), channel_id=1, source_target_pairs={{0,1},{1,0},{2,3},{3,2},{4,5},{5,4},{6,7},{7,6},{8,9},{9,8},{10,11... | collective-permute-start | bytes 6291464 | tf_op jit(solution)/shard_map/ppermute | solution.py:107
  2.1 15.2 %collective-permute-start.1 = (bf16[2,128,1024]{2,1,0:T(8,128)(2,1)}, bf16[2,128,1024]{2,1,0:T(8,128)(2,1)}, u32[]{:S(2)}, u32[]{:S(2)}) collective-permute-start(bf16[2,128,1024]{2,1,0:T(8,128)(2,1)} %constant_dynamic-slice_fusion), channel_id=1, source_target_pairs={{0,63},{1,2},{2,1},{3,4},{4,3},{5,6},{6,5},{7,8},{8,7},{9,10},{10,... | collective-permute-start | bytes 1572872 | tf_op jit(solution)/shard_map/ppermute | solution.py:104
  12.3 17.8 %collective-permute-start.3 = (bf16[4,128,1024]{2,1,0:T(8,128)(2,1)}, bf16[4,128,1024]{2,1,0:T(8,128)(2,1)S(1)}, u32[]{:S(2)}, u32[]{:S(2)}) collective-permute-start(bf16[4,128,1024]{2,1,0:T(8,128)(2,1)} %constant_dynamic-slice_fusion.1), channel_id=1, source_target_pairs={{0,63},{1,2},{2,1},{3,4},{4,3},{5,6},{6,5},{7,8},{8,7},{9,10},{10,... | collective-permute-start | bytes 3145736 | tf_op jit(solution)/shard_map/ppermute | solution.py:106
  17.2 9.5 %collective-permute-start.2 = (bf16[2,128,1024]{2,1,0:T(8,128)(2,1)}, bf16[2,128,1024]{2,1,0:T(8,128)(2,1)}, u32[]{:S(2)}, u32[]{:S(2)}) collective-permute-start(bf16[2,128,1024]{2,1,0:T(8,128)(2,1)} %collective-permute-done.1.near), channel_id=1, source_target_pairs={{0,64},{1,193},{2,66},{3,195},{4,68},{5,197},{6,70},{7,199},{8,72}... | collective-permute-start | bytes 1572872 | tf_op jit(solution)/shard_map/ppermute | solution.py:108

commit v2 on v0

v2 whole, which is shorter than its diff:
```python
import jax
import jax.numpy as jnp
from jax import lax
from jax.experimental import pallas as pl
from jax.experimental.pallas import tpu as pltpu
from jax.sharding import PartitionSpec as P

ROWS = 8
HALF = ROWS // 2
LISTED = 8
BS = 128
SPAN = LISTED * BS
WINDOW = 3 * ROWS
STRIDE = WINDOW + 1
ZERO = WINDOW
COLUMNS = 5 * ROWS
ANY = pl.BlockSpec(memory_space=pl.ANY)
HBM = pl.BlockSpec(memory_space=pltpu.HBM)
SMEM = pl.BlockSpec(memory_space=pltpu.SMEM)
VMEM = pl.BlockSpec(memory_space=pltpu.VMEM)


def tables(pattern, grid_index):
    blocks = pattern.shape[0]
    first = grid_index * ROWS
    ring = jnp.concatenate([pattern[-ROWS:], pattern, pattern[:ROWS]], axis=0)
    window = lax.dynamic_slice_in_dim(ring, first, WINDOW, 0)
    rel = window - first + 2 * ROWS
    rel = jnp.where(rel >= blocks // 2, rel - blocks, rel)
    rel = jnp.where(rel < -blocks // 2, rel + blocks, rel)
    listed = rel[ROWS : 2 * ROWS] - ROWS
    rows = lax.broadcasted_iota(jnp.int32, (STRIDE, COLUMNS), 0)
    cols = lax.broadcasted_iota(jnp.int32, (STRIDE, COLUMNS), 1)
    padded = jnp.concatenate([rel, jnp.full((1, LISTED), -1, jnp.int32)], axis=0)
    place = jnp.full((STRIDE, COLUMNS), ZERO, jnp.int32)
    for b in range(LISTED):
        place = jnp.where(padded[:, b : b + 1] == cols, b * STRIDE + rows, place)
    return listed.reshape(-1), place.reshape(-1)


def pick_kernel(count, near, source, out, sem):
    parity = lax.rem(lax.axis_index("grid"), 2)
    if near:
        start = HALF * parity + count * lax.rem(lax.axis_index("layer"), 2)
    else:
        start = HALF * (1 - parity)
    copy = pltpu.make_async_copy(source.at[pl.ds(start, count)], out, sem)
    copy.start()
    copy.wait()


def pick(density, count, near):
    return pl.pallas_call(
        lambda *refs: pick_kernel(count, near, *refs),
        out_shape=jax.ShapeDtypeStruct((count, BS, SPAN), density.dtype),
        in_specs=[HBM],
        out_specs=ANY,
        scratch_shapes=[pltpu.SemaphoreType.DMA],
        compiler_params=pltpu.CompilerParams(vmem_limit_bytes=2**20),
        name="pick_near" if near else "pick_far",
    )(density)


def place_rows(source, count, store, first, sem):
    return [
        pltpu.make_async_copy(
            source.at[:, :, pl.ds(s * BS, BS)], store.at[pl.ds(s * STRIDE + first, count)], sem.at[s]
        )
        for s in range(LISTED)
    ]


class Blocks:
    def __init__(self, listed, place, store, i):
        self.listed, self.place, self.store, self.i = listed, place, store, i

    def row(self, c):
        return self.listed[self.i * LISTED + c]

    def block(self, row, a):
        return self.store[self.place[row * COLUMNS + self.row(a) + ROWS]]

    def pair(self, row, a):
        return jnp.concatenate([self.block(row, a), self.block(row, a + 1)], axis=1)

    def times(self, left, rows, a):
        total = jnp.zeros((BS, 2 * BS), jnp.float32)
        for c in range(0, LISTED, 2):
            right = jnp.concatenate([self.pair(rows[c], a), self.pair(rows[c + 1], a)], axis=0)
            total += jnp.dot(left(c), right, preferred_element_type=jnp.float32)
        return total


def add_rows(blocks, own, i, low, total):
    for c in range(LISTED):
        row = blocks.row(c)

        @pl.when(jnp.logical_and(row >= low, row < low + HALF))
        def _():
            left = own[i, :, c * BS : (c + 1) * BS]
            for a in range(0, LISTED, 2):
                total[:, a * BS : (a + 2) * BS] += jnp.dot(
                    left, blocks.pair(row, a), preferred_element_type=jnp.float32
                )


def finish(blocks, total, square, result):
    layer = lax.axis_index("layer")
    square[...] = total[...].astype(jnp.bfloat16)
    rows = [blocks.row(c) for c in range(LISTED)]
    cube = blocks.times(lambda c: square[:, c * BS : (c + 2) * BS], rows, 2 * layer)
    start = pl.multiple_of(layer * 2 * BS, 2 * BS)
    result[...] = 3.0 * square[:, pl.ds(start, 2 * BS)].astype(jnp.float32) - 2.0 * cube


def close_kernel(listed, place, own, inner, store, partial, sems):
    parity = lax.rem(lax.axis_index("grid"), 2)
    outer = 2 * ROWS * parity
    copies = place_rows(own, ROWS, store, ROWS, sems.at[0])
    copies += place_rows(inner, ROWS, store, 2 * ROWS - outer, sems.at[1])
    for copy in copies:
        copy.start()
    store[ZERO] = jnp.zeros((BS, BS), jnp.bfloat16)
    for copy in copies:
        copy.wait()

    def one_row(i, carry):
        blocks = Blocks(listed, place, store, i)
        rows = []
        for c in range(LISTED):
            row = blocks.row(c)
            away = jnp.logical_and(row >= outer, row < outer + ROWS)
            rows.append(jnp.where(away, WINDOW, row))
        for a in range(0, LISTED, 2):
            partial[i, :, a * BS : (a + 2) * BS] = blocks.times(
                lambda c: own[i, :, c * BS : (c + 2) * BS], rows, a
            )
        return carry

    lax.fori_loop(0, ROWS, one_row, 0)


def near_kernel(listed, place, own, near, swapped, partial, _, store, rest, out, total, square, result, sems, out_sems):
    parity = lax.rem(lax.axis_index("grid"), 2)
    half = lax.rem(lax.axis_index("layer"), 2)
    low = 2 * ROWS * parity + HALF * (1 - parity)
    copies = place_rows(near, 2, store, low + 2 * half, sems.at[0])
    copies += place_rows(swapped, 2, store, low + 2 * (1 - half), sems.at[1])
    for copy in copies:
        copy.start()
    for copy in copies:
        copy.wait()

    def unfinished(e, carry):
        i = jnp.where(parity == 0, e, ROWS - 1 - e)
        rest[e] = partial[i]
        add_rows(Blocks(listed, place, store, i), own, i, low, rest.at[e])
        return carry

    def finished(e, carry):
        i = jnp.where(parity == 0, e, ROWS - 1 - e)
        blocks = Blocks(listed, place, store, i)
        total[...] = partial[i]
        add_rows(blocks, own, i, low, total)
        finish(blocks, total, square, result.at[e - HALF])
        pltpu.make_async_copy(result.at[e - HALF], out.at[i], out_sems.at[e - HALF]).start()
        return carry

    lax.fori_loop(HALF, ROWS, finished, 0)
    lax.fori_loop(0, HALF, unfinished, 0)
    for e in range(HALF):
        pltpu.make_async_copy(result.at[e], out.at[0], out_sems.at[e]).wait()


def far_kernel(listed, place, own, far, rest, _s, _o, store, out, total, square, result, sems, out_sems):
    parity = lax.rem(lax.axis_index("grid"), 2)
    low = 2 * ROWS * parity + HALF * parity
    copies = place_rows(far, HALF, store, low, sems)
    for copy in copies:
        copy.start()
    for copy in copies:
        copy.wait()

    def one_row(e, carry):
        i = jnp.where(parity == 0, e, ROWS - 1 - e)
        blocks = Blocks(listed, place, store, i)
        total[...] = rest[e]
        add_rows(blocks, own, i, low, total)
        finish(blocks, total, square, result.at[e])
        pltpu.make_async_copy(result.at[e], out.at[i], out_sems.at[e]).start()
        return carry

    lax.fori_loop(0, HALF, one_row, 0)
    for e in range(HALF):
        pltpu.make_async_copy(result.at[e], out.at[0], out_sems.at[e]).wait()


def local(density, pattern):
    grid = lax.axis_size("grid")
    layers = lax.axis_size("layer")
    outer_pairs = [(i, (i - 1) % grid if i % 2 == 0 else (i + 1) % grid) for i in range(grid)]
    inner_pairs = [(i, i + 1 if i % 2 == 0 else i - 1) for i in range(grid)]
    swap_pairs = []
    for y in range(layers):
        for i in range(grid):
            other = (y ^ 1) if i % 2 == 0 else ((y + 1) ^ 1) - 1
            swap_pairs.append((y * grid + i, (other % layers) * grid + i))
    inner = lax.ppermute(density, "grid", inner_pairs)
    near = lax.ppermute(pick(density, 2, True), "grid", outer_pairs)
    far = lax.ppermute(pick(density, HALF, False), "grid", outer_pairs)
    swapped = lax.ppermute(near, ("layer", "grid"), swap_pairs)
    listed, place = tables(pattern, lax.axis_index("grid"))

    store_shape = jax.ShapeDtypeStruct((LISTED * STRIDE, BS, BS), jnp.bfloat16)
    out_shape = jax.ShapeDtypeStruct((ROWS, BS, 2 * BS), jnp.float32)
    limits = pltpu.CompilerParams(vmem_limit_bytes=8 * 2**20)
    working = [
        pltpu.VMEM((BS, SPAN), jnp.float32),
        pltpu.VMEM((BS, SPAN), jnp.bfloat16),
        pltpu.VMEM((HALF, BS, 2 * BS), jnp.float32),
    ]
    store, partial = pl.pallas_call(
        close_kernel,
        out_shape=(store_shape, jax.ShapeDtypeStruct((ROWS, BS, SPAN), jnp.float32)),
        in_specs=[SMEM, SMEM, VMEM, VMEM],
        out_specs=(VMEM, VMEM),
        scratch_shapes=[pltpu.SemaphoreType.DMA((2, LISTED))],
        compiler_params=limits,
        cost_estimate=pl.CostEstimate(flops=4_000_000_000, bytes_accessed=8_000_000, transcendentals=0),
        name="close",
    )(listed, place, density, inner)
    store, rest, out = pl.pallas_call(
        near_kernel,
        out_shape=(store_shape, jax.ShapeDtypeStruct((HALF, BS, SPAN), jnp.float32), out_shape),
        in_specs=[SMEM, SMEM, VMEM, VMEM, VMEM, VMEM, VMEM],
        out_specs=(VMEM, VMEM, ANY),
        scratch_shapes=working
        + [pltpu.SemaphoreType.DMA((2, LISTED)), pltpu.SemaphoreType.DMA((HALF,))],
        input_output_aliases={6: 0},
        compiler_params=limits,
        cost_estimate=pl.CostEstimate(flops=2_000_000_000, bytes_accessed=4_000_000, transcendentals=0),
        name="near",
    )(listed, place, density, near, swapped, partial, store)
    return pl.pallas_call(
        far_kernel,
        out_shape=(store_shape, out_shape),
        in_specs=[SMEM, SMEM, VMEM, VMEM, VMEM, VMEM, ANY],
        out_specs=(VMEM, ANY),
        scratch_shapes=working
        + [pltpu.SemaphoreType.DMA((LISTED,)), pltpu.SemaphoreType.DMA((HALF,))],
        input_output_aliases={5: 0, 6: 1},
        compiler_params=limits,
        cost_estimate=pl.CostEstimate(flops=1_000_000_000, bytes_accessed=4_000_000, transcendentals=0),
        name="far",
    )(listed, place, density, far, rest, store, out)[1]


def solution(mesh):
    placed = (P("grid", None, None), P())
    return jax.shard_map(
        local, mesh=mesh, in_specs=placed, out_specs=P("grid", None, "layer"), check_vma=False
    )
```

time: 280 us -> 37.6 us (0.13); the launches traced: 277 us -> 37.4 us
  waiting for transfers between devices: 119 us -> 5.49 us
  blocking collectives: 71.5 us -> 0 us
  local copies, waits for them, and re-layouts: 47.8 us -> 3.5 us
  Pallas kernels: 0 us -> 18.3 us
  between operations: 14.2 us -> 0.1 us
  matrix products: 12.9 us -> 0 us
  other arithmetic: 3.91 us -> 0.3 us
    unnamed x2 -> x0, waiting for transfers between devices: 101 us -> none
    unnamed x1 -> x0, blocking collectives: 71.5 us -> none
    gather x9 -> x0, local copies, waits for them, and re-layouts: 28 us -> none  [the longest x8 27.4 us: align_row(): fetched = jnp.take(padded_blocks, row_places, axis=0)]
    pallas_call x0 -> x5, Pallas kernels: none -> 18.3 us  [the longest x1 6.54 us: local(): pl.pallas_call(close_kernel, out_shape=(store_shape, jax.ShapeDtypeStruct...]
    dot_general x10 -> x0, matrix products: 12.9 us -> none  [the longest x1 5.07 us: local(): jnp.einsum('ixay,iayjz->ixjz', left_slots, aligned, preferred_element_typ...]
    ppermute x2 -> x4, waiting for transfers between devices: 17.4 us -> 5.49 us  [the longest x1 4.06 us: local(): near = lax.ppermute(pick(density, 2, True), 'grid', outer_pairs)]
    dynamic_update_slice x8 -> x0, local copies, waits for them, and re-layouts: 7.35 us -> none  [local(): aligned = lax.map(align_row, (located, selector))]
    unnamed x12 -> x8, local copies, waits for them, and re-layouts: 10.3 us -> 3.19 us
  transfers between devices with their start and end apart: 3 -> 4, of which waited for: 2 -> 2; matrix products, arithmetic and copies ran while one was open for 2% -> 2% of each run, Pallas kernels for 0% -> 38%
where the time goes in v2:
time: 37.6 us; the launch traced here: 37.4 us
  Pallas kernels  18.3 us (49%)
  starting transfers between devices  9.64 us (26%)
  waiting for transfers between devices  5.49 us (15%)
  local copies, waits for them, and re-layouts  3.5 us (9%)
    ppermute x1, starting transfers between devices, local(): near = lax.ppermute(pick(density, 2, True), 'grid', outer_pairs)  8.25 us
    pallas_call x1, Pallas kernels, local(): pl.pallas_call(close_kernel, out_shape=(store_shape, jax.ShapeDtypeStruct...  6.54 us
    pallas_call x1, Pallas kernels, local(): pl.pallas_call(near_kernel, out_shape=(store_shape, jax.ShapeDtypeStruct(...  6.01 us
    ppermute x1, waiting for transfers between devices, local(): near = lax.ppermute(pick(density, 2, True), 'grid', outer_pairs)  4.06 us
    pallas_call x1, Pallas kernels, local(): pl.pallas_call(far_kernel, out_shape=(store_shape, out_shape), in_specs=[...  4 us
    unnamed x8, local copies, waits for them, and re-layouts  3.19 us
    pallas_call x2, Pallas kernels, pick(): pl.pallas_call(lambda *refs: pick_kernel(count, near, *refs), out_shape=j...  1.78 us
    ppermute x1, waiting for transfers between devices, local(): swapped = lax.ppermute(near, ('layer', 'grid'), swap_pairs)  1.43 us
  transfers between devices with their start and end apart: 4, of which 2 were waited for; matrix products, arithmetic and copies ran while one was open for 2% of the time, Pallas kernels for 38%

profile of v2, /device:TPU:16, one launch (start us, length us, event | category | flops | bytes accessed | tf_op | source)
XLA Modules:
  0.0 37.4 jit_solution(7748742232423669799)
XLA Ops:
  0.0 0.0 collective-permute-start.3
  0.0 0.0 copy-start
  0.0 1.6 %copy-done = bf16[8,128,1024]{2,1,0:T(8,128)(2,1)S(1)} copy-done((bf16[8,128,1024]{2,1,0:T(8,128)(2,1)S(1)}, bf16[8,128,1024]{2,1,0:T(8,128)(2,1)}, u32[]{:S(2)}) %copy-start) | copy-done | bytes 2097176
  1.6 0.0 copy-start.3
  1.6 0.0 copy-start.2
  1.6 0.8 %pick_near.1 = bf16[2,128,1024]{2,1,0:T(8,128)(2,1)} custom-call(bf16[8,128,1024]{2,1,0:T(8,128)(2,1)S(1)} %copy-done), custom_call_target="tpu_custom_call" | custom-call | tf_op jit(solution)/shard_map/pick_near/pallas_call | solution.py:53
  2.4 8.2 %collective-permute-start.1 = (bf16[2,128,1024]{2,1,0:T(8,128)(2,1)}, bf16[2,128,1024]{2,1,0:T(8,128)(2,1)}, u32[]{:S(2)}, u32[]{:S(2)}) collective-permute-start(bf16[2,128,1024]{2,1,0:T(8,128)(2,1)} %pick_near.1), channel_id=1, source_target_pairs={{0,63},{1,2},{2,1},{3,4},{4,3},{5,6},{6,5},{7,8},{8,7},{9,10},{10,... | collective-permute-start | bytes 1572872 | tf_op jit(solution)/shard_map/ppermute | solution.py:209
  10.7 0.0 copy-start.1
  10.7 1.6 %copy-done.1 = bf16[8,128,1024]{2,1,0:T(8,128)(2,1)S(1)} copy-done((bf16[8,128,1024]{2,1,0:T(8,128)(2,1)S(1)}, bf16[8,128,1024]{2,1,0:T(8,128)(2,1)}, u32[]{:S(2)}) %copy-start.1) | copy-done | bytes 2097176
  12.2 1.0 %pick_far.1 = bf16[4,128,1024]{2,1,0:T(8,128)(2,1)} custom-call(bf16[8,128,1024]{2,1,0:T(8,128)(2,1)S(1)} %copy-done.1), custom_call_target="tpu_custom_call" | custom-call | tf_op jit(solution)/shard_map/pick_far/pallas_call | solution.py:53
  13.2 0.1 collective-permute-start
  13.4 0.0 copy-done.3
  13.4 0.1 fusion.11
  13.4 0.1 compare_select_fusion
  13.6 0.1 select_select_fusion
  13.7 0.1 reshape.45.place
  13.8 4.1 %collective-permute-done.1.near = bf16[2,128,1024]{2,1,0:T(8,128)(2,1)} collective-permute-done((bf16[2,128,1024]{2,1,0:T(8,128)(2,1)}, bf16[2,128,1024]{2,1,0:T(8,128)(2,1)}, u32[]{:S(2)}, u32[]{:S(2)}) %collective-permute-start.1) | collective-permute-done | bytes 524320 | tf_op jit(solution)/shard_map/ppermute | solution.py:209
  17.8 1.3 %collective-permute-start.2 = (bf16[2,128,1024]{2,1,0:T(8,128)(2,1)}, bf16[2,128,1024]{2,1,0:T(8,128)(2,1)}, u32[]{:S(2)}, u32[]{:S(2)}) collective-permute-start(bf16[2,128,1024]{2,1,0:T(8,128)(2,1)} %collective-permute-done.1.near), channel_id=1, source_target_pairs={{0,64},{1,193},{2,66},{3,195},{4,68},{5,197},{6,70},{7,199},{8,72}... | collective-permute-start | bytes 1572872 | tf_op jit(solution)/shard_map/ppermute | solution.py:211
  19.1 0.1 slice_add_fusion
  19.2 0.1 copy.6
  19.3 0.1 reshape.40.listed
  19.4 0.0 collective-permute-done.3.inner
  19.4 0.0 copy-done.2
  19.4 6.5 %close.1 = (bf16[200,128,128]{2,1,0:T(8,128)(2,1)S(1)}, f32[8,128,1024]{2,1,0:T(8,128)S(1)}) custom-call(s32[64]{0:T(128)S(1)} %reshape.40.listed, s32[1000]{0:T(1024)S(1)} %reshape.45.place, bf16[8,128,1024]{2,1,0:T(8,128)(2,1)S(1)} %copy-done.2, bf16[8,128,1024]{2,1,0:T(8,128)(2,1)} %collective-permute-done.3.inner), custom_call_target="tpu_custom_call" | custom-call | flops 4000000000 | bytes 8000000 | tf_op jit(solution)/shard_map/close/pallas_call | solution.py:222
  25.9 1.4 %collective-permute-done.2.swapped = bf16[2,128,1024]{2,1,0:T(8,128)(2,1)} collective-permute-done((bf16[2,128,1024]{2,1,0:T(8,128)(2,1)}, bf16[2,128,1024]{2,1,0:T(8,128)(2,1)}, u32[]{:S(2)}, u32[]{:S(2)}) %collective-permute-start.2) | collective-permute-done | bytes 524320 | tf_op jit(solution)/shard_map/ppermute | solution.py:211
  27.3 6.0 %near.1 = (bf16[200,128,128]{2,1,0:T(8,128)(2,1)S(1)}, f32[4,128,1024]{2,1,0:T(8,128)S(1)}, f32[8,128,256]{2,1,0:T(8,128)}) custom-call(s32[64]{0:T(128)S(1)} %reshape.40.listed, s32[1000]{0:T(1024)S(1)} %reshape.45.place, bf16[8,128,1024]{2,1,0:T(8,128)(2,1)S(1)} %copy-done.2, ...), custom_call_target="tpu_custom_call", output_to_operand_aliasing={{0}: (6, {})} | custom-call | flops 2000000000 | bytes 4000000 | tf_op jit(solution)/shard_map/near/pallas_call | solution.py:232
  33.4 0.0 collective-permute-done.far
  33.4 4.0 %far.1 = (bf16[200,128,128]{2,1,0:T(8,128)(2,1)S(1)}, f32[8,128,256]{2,1,0:T(8,128)}) custom-call(s32[64]{0:T(128)S(1)} %reshape.40.listed, s32[1000]{0:T(1024)S(1)} %reshape.45.place, bf16[8,128,1024]{2,1,0:T(8,128)(2,1)S(1)} %copy-done.2, bf16[4,128,1024]{2,1,0:T(8,128)(2,1)S(1)} %collective-permute-done.far, ...), custom_call_target="tpu_custom_call", output_to_operand_aliasing={{0}: (5, {}), {1}: (6, {})} | custom-call | flops 1000000000 | bytes 4000000 | tf_op jit(solution)/shard_map/far/pallas_call | solution.py:244
  (5 shorter events, 0.0 us)
Async XLA Ops:
  0.0 19.4 %collective-permute-start.3 = (bf16[8,128,1024]{2,1,0:T(8,128)(2,1)}, bf16[8,128,1024]{2,1,0:T(8,128)(2,1)}, u32[]{:S(2)}, u32[]{:S(2)}) collective-permute-start(bf16[8,128,1024]{2,1,0:T(8,128)(2,1)} %own.5), channel_id=1, source_target_pairs={{0,1},{1,0},{2,3},{3,2},{4,5},{5,4},{6,7},{7,6},{8,9},{9,8},{10,11... | collective-permute-start | bytes 6291464 | tf_op jit(solution)/shard_map/ppermute | solution.py:208
  0.0 1.6 %copy-start = (bf16[8,128,1024]{2,1,0:T(8,128)(2,1)S(1)}, bf16[8,128,1024]{2,1,0:T(8,128)(2,1)}, u32[]{:S(2)}) copy-start(bf16[8,128,1024]{2,1,0:T(8,128)(2,1)} %own.5) | copy-start | bytes 6291460
  1.6 11.8 %copy-start.3 = (s32[512,8]{0,1:T(8,128)S(1)}, s32[512,8]{0,1:T(8,128)}, u32[]{:S(2)}) copy-start(s32[512,8]{0,1:T(8,128)} %param.3) | copy-start | bytes 49156
  1.6 17.8 %copy-start.2 = (bf16[8,128,1024]{2,1,0:T(8,128)(2,1)S(1)}, bf16[8,128,1024]{2,1,0:T(8,128)(2,1)}, u32[]{:S(2)}) copy-start(bf16[8,128,1024]{2,1,0:T(8,128)(2,1)} %own.5) | copy-start | bytes 6291460
  2.4 15.4 %collective-permute-start.1 = (bf16[2,128,1024]{2,1,0:T(8,128)(2,1)}, bf16[2,128,1024]{2,1,0:T(8,128)(2,1)}, u32[]{:S(2)}, u32[]{:S(2)}) collective-permute-start(bf16[2,128,1024]{2,1,0:T(8,128)(2,1)} %pick_near.1), channel_id=1, source_target_pairs={{0,63},{1,2},{2,1},{3,4},{4,3},{5,6},{6,5},{7,8},{8,7},{9,10},{10,... | collective-permute-start | bytes 1572872 | tf_op jit(solution)/shard_map/ppermute | solution.py:209
  10.7 1.6 %copy-start.1 = (bf16[8,128,1024]{2,1,0:T(8,128)(2,1)S(1)}, bf16[8,128,1024]{2,1,0:T(8,128)(2,1)}, u32[]{:S(2)}) copy-start(bf16[8,128,1024]{2,1,0:T(8,128)(2,1)} %own.5) | copy-start | bytes 6291460
  13.2 20.1 %collective-permute-start = (bf16[4,128,1024]{2,1,0:T(8,128)(2,1)}, bf16[4,128,1024]{2,1,0:T(8,128)(2,1)S(1)}, u32[]{:S(2)}, u32[]{:S(2)}) collective-permute-start(bf16[4,128,1024]{2,1,0:T(8,128)(2,1)} %pick_far.1), channel_id=1, source_target_pairs={{0,63},{1,2},{2,1},{3,4},{4,3},{5,6},{6,5},{7,8},{8,7},{9,10},{10,... | collective-permute-start | bytes 3145736 | tf_op jit(solution)/shard_map/ppermute | solution.py:210
  17.8 9.5 %collective-permute-start.2 = (bf16[2,128,1024]{2,1,0:T(8,128)(2,1)}, bf16[2,128,1024]{2,1,0:T(8,128)(2,1)}, u32[]{:S(2)}, u32[]{:S(2)}) collective-permute-start(bf16[2,128,1024]{2,1,0:T(8,128)(2,1)} %collective-permute-done.1.near), channel_id=1, source_target_pairs={{0,64},{1,193},{2,66},{3,195},{4,68},{5,197},{6,70},{7,199},{8,72}... | collective-permute-start | bytes 1572872 | tf_op jit(solution)/shard_map/ppermute | solution.py:211

commit v3 on v0

v3 whole, which is shorter than its diff:
```python
import jax
import jax.numpy as jnp
import numpy as np
from jax import lax
from jax.experimental import pallas as pl
from jax.experimental.pallas import tpu as pltpu
from jax.sharding import PartitionSpec as P

ROWS = 8
LISTED = 8
BS = 128
SPAN = LISTED * BS
WINDOW = 3 * ROWS
FAR = 4
NEAR = ROWS - FAR
SHARE = NEAR * LISTED // 2
INNER_AT = ROWS * LISTED
NEAR_AT = 2 * ROWS * LISTED
FAR_AT = NEAR_AT + NEAR * LISTED
ZERO = FAR_AT + FAR * LISTED
STORE = ZERO + 1

ANY = pl.BlockSpec(memory_space=pl.ANY)
HBM = pl.BlockSpec(memory_space=pltpu.HBM)
SMEM = pl.BlockSpec(memory_space=pltpu.SMEM)
VMEM = pl.BlockSpec(memory_space=pltpu.VMEM)


def places(odd):
    rows = []
    for w in range(FAR):
        rows.append([FAR_AT + w * LISTED + s for s in range(LISTED)])
    for w in range(FAR, ROWS):
        rows.append([NEAR_AT + (w - FAR) * LISTED + s for s in range(LISTED)])
    for base in (0, INNER_AT):
        for e in range(ROWS):
            i = ROWS - 1 - e if odd else e
            rows.append([base + s * ROWS + i for s in range(LISTED)])
    rows.append([ZERO] * LISTED)
    return np.array(rows, np.int32)


def tables(pattern):
    blocks = pattern.shape[0]
    g = lax.axis_index("grid")
    odd = g % 2 == 1
    first = g * ROWS - ROWS
    ring = jnp.concatenate([pattern[-ROWS:], pattern, pattern[:ROWS]], axis=0)
    columns = lax.dynamic_slice_in_dim(ring, g * ROWS, WINDOW, 0) - first
    columns = jnp.where(columns >= blocks, columns - blocks, columns)
    columns = jnp.where(columns < 0, columns + blocks, columns)
    columns = jnp.where(odd, WINDOW - 1 - columns[::-1], columns)
    listed = columns[ROWS : 2 * ROWS]
    columns = jnp.concatenate([columns, jnp.full((1, LISTED), -1, jnp.int32)], axis=0)
    at = jnp.where(odd, places(True), places(False))
    xs = lax.broadcasted_iota(jnp.int32, (WINDOW + 1, WINDOW), 1)
    place = jnp.full((WINDOW + 1, WINDOW), ZERO, jnp.int32)
    for s in range(LISTED):
        place = jnp.where(columns[:, s : s + 1] == xs, at[:, s : s + 1], place)
    return listed.reshape(-1), place.reshape(-1)


def parity():
    return lax.rem(lax.axis_index("grid"), 2)


def half():
    return lax.rem(lax.axis_index("layer"), 2)


def row_of(e):
    return jnp.where(parity() == 0, e, ROWS - 1 - e)


def sent_row(w):
    return jnp.where(parity() == 1, w, ROWS - 1 - w)


def pick_kernel(source, out, sems):
    copies = []
    for n in range(SHARE):
        row = sent_row(FAR + (NEAR // 2) * half() + n // LISTED)
        block = source.at[row, :, pl.ds(n % LISTED * BS, BS)]
        copies.append(pltpu.make_async_copy(block, out.at[n], sems.at[n]))
    for copy in copies:
        copy.start()
    for copy in copies:
        copy.wait()


def pick_far_kernel(source, out, sems):
    copies = []
    for n in range(FAR * LISTED):
        block = source.at[sent_row(n // LISTED), :, pl.ds(n % LISTED * BS, BS)]
        copies.append(pltpu.make_async_copy(block, out.at[n], sems.at[n]))
    for copy in copies:
        copy.start()
    for copy in copies:
        copy.wait()


class Blocks:
    def __init__(self, listed, place, store, e):
        self.listed, self.place, self.store, self.e = listed, place, store, e

    def row(self, c):
        return self.listed[self.e * LISTED + c]

    def block(self, row, a):
        return self.store[self.place[row * WINDOW + self.row(a)]]

    def pair(self, row, a):
        return jnp.concatenate([self.block(row, a), self.block(row, a + 1)], axis=1)

    def tile(self, row0, row1, a):
        return jnp.concatenate([self.pair(row0, a), self.pair(row1, a)], axis=0)

    def times(self, left, rows, a):
        total = jnp.zeros((BS, 2 * BS), jnp.float32)
        for c in range(0, LISTED, 2):
            right = self.tile(rows[c], rows[c + 1], a)
            total += jnp.dot(left(c), right, preferred_element_type=jnp.float32)
        return total


def close_rows(listed, place, own, store, partial, first):
    def one_row(n, carry):
        e = first + n
        blocks = Blocks(listed, place, store, e)
        i = row_of(e)
        rows = []
        for c in range(LISTED):
            row = blocks.row(c)
            rows.append(jnp.where(row < ROWS, WINDOW, row))
        for a in range(0, LISTED, 2):
            partial[n, :, a * BS : (a + 2) * BS] = blocks.times(
                lambda c: own[i, :, c * BS : (c + 2) * BS], rows, a
            )
        return carry

    lax.fori_loop(0, ROWS // 2, one_row, 0)


def close_kernel(listed, place, own, inner, store, partial):
    for n, source in enumerate((own, inner)):
        for r in range(ROWS):
            for s in range(LISTED):
                store[n * INNER_AT + s * ROWS + r] = source[r, :, s * BS : (s + 1) * BS]
    store[ZERO] = jnp.zeros((BS, BS), jnp.bfloat16)
    close_rows(listed, place, own, store, partial, 0)


def close_kernel2(listed, place, own, store, partial):
    close_rows(listed, place, own, store, partial, ROWS // 2)


def chosen(blocks, low, high, index, most):
    base = blocks.e * LISTED
    for t in range(LISTED):
        index[base + t] = 0
    count = jnp.int32(0)
    for c in range(LISTED):
        row = blocks.row(c)
        index[base + count] = c
        count += jnp.logical_and(row >= low, row < high).astype(jnp.int32)
    picks = []
    for t in range(most):
        valid = t < count
        c = jnp.where(valid, index[base + t], 0)
        picks.append((c, jnp.where(valid, blocks.row(c), WINDOW)))
    return count, picks


def step(blocks, own, picks, a):
    i = row_of(blocks.e)
    left = jnp.concatenate(
        [own[i, :, pl.ds(pl.multiple_of(c * BS, BS), BS)] for c, _ in picks], axis=1
    )
    right = blocks.tile(picks[0][1], picks[1][1], a)
    return jnp.dot(left, right, preferred_element_type=jnp.float32)


def add_rows(listed, place, store, own, source, total, rows, low, high, mosts, index):
    later = []
    for e, most in zip(rows, mosts):
        blocks = Blocks(listed, place, store, e)
        count, picks = chosen(blocks, low, high, index, most)
        for a in range(0, LISTED, 2):
            cols = slice(a * BS, (a + 2) * BS)
            total[e - rows[0], :, cols] = source(e)[:, cols] + step(blocks, own, picks[:2], a)
        for t in range(2, most, 2):
            later.append((blocks, count, picks[t : t + 2], t))
    for blocks, count, picks, t in later:

        @pl.when(count > t)
        def _():
            for a in range(0, LISTED, 2):
                cols = slice(a * BS, (a + 2) * BS)
                total[blocks.e - rows[0], :, cols] += step(blocks, own, picks, a)


def finish(listed, place, store, total, rows, square, result, out, sems):
    layer = lax.axis_index("layer")
    start = pl.multiple_of(layer * 2 * BS, 2 * BS)
    copies = []
    for e in rows:
        n = e - rows[0]
        blocks = Blocks(listed, place, store, e)
        square[n] = total[n].astype(jnp.bfloat16)
        cube = blocks.times(
            lambda c: square[n, :, c * BS : (c + 2) * BS],
            [blocks.row(c) for c in range(LISTED)],
            2 * layer,
        )
        result[n] = 3.0 * square[n, :, pl.ds(start, 2 * BS)].astype(jnp.float32) - 2.0 * cube
        copies.append(pltpu.make_async_copy(result.at[n], out.at[row_of(e)], sems.at[n]))
        copies[-1].start()
    for copy in copies:
        copy.wait()


def insert(pieces, store, sems):
    copies = [
        pltpu.make_async_copy(piece, store.at[pl.ds(at, count)], sems.at[n])
        for n, (piece, at, count) in enumerate(pieces)
    ]
    for copy in copies:
        copy.start()
    for copy in copies:
        copy.wait()


def share_low(mine):
    return FAR + NEAR // 2 * (half() if mine else 1 - half())


def near_kernel(listed, place, own, near, partial, partial2, _, store, sums, index, sems):
    insert([(near, NEAR_AT + SHARE * half(), SHARE)], store, sems)
    low = share_low(True)
    source = lambda e: partial.at[e] if e < ROWS // 2 else partial2.at[e - ROWS // 2]
    add_rows(
        listed, place, store, own, source, sums, list(range(ROWS)), low, low + 2, [2] * ROWS, index
    )


def swapped_kernel(
    listed, place, own, swapped, sums, _, store, rest, out, total, square, result, index, sems, out_sems
):
    insert([(swapped, NEAR_AT + SHARE * (1 - half()), SHARE)], store, sems)
    low = share_low(False)
    source = lambda e: sums.at[e]
    ended, left = list(range(FAR, ROWS)), list(range(FAR))
    add_rows(listed, place, store, own, source, total, ended, low, low + 2, [2] * NEAR, index)
    add_rows(listed, place, store, own, source, rest, left, low, low + 2, [2] * FAR, index)
    finish(listed, place, store, total, ended, square, result, out, out_sems)


def far_kernel(
    listed, place, own, far, rest, _s, _o, store, out, total, square, result, index, sems, out_sems
):
    insert([(far, FAR_AT, FAR * LISTED)], store, sems)
    source = lambda e: rest.at[e]
    rows = list(range(FAR))
    add_rows(listed, place, store, own, source, total, rows, 0, FAR, [4, 4, 2, 2], index)
    finish(listed, place, store, total, rows, square, result, out, out_sems)


def shape(*dims, dtype=jnp.bfloat16):
    return jax.ShapeDtypeStruct(dims, dtype)


def cost(flops):
    return pl.CostEstimate(flops=flops, bytes_accessed=4_000_000, transcendentals=0)


def local(density, pattern):
    grid = lax.axis_size("grid")
    layers = lax.axis_size("layer")
    outer_pairs = [(i, (i - 1) % grid if i % 2 == 0 else (i + 1) % grid) for i in range(grid)]
    inner_pairs = [(i, i + 1 if i % 2 == 0 else i - 1) for i in range(grid)]
    swap_pairs = []
    for y in range(layers):
        for i in range(grid):
            other = (y ^ 1) if i % 2 == 0 else ((y + 1) ^ 1) - 1
            swap_pairs.append((y * grid + i, (other % layers) * grid + i))
    small = pltpu.CompilerParams(vmem_limit_bytes=8 * 2**20)
    limits = pltpu.CompilerParams(vmem_limit_bytes=24 * 2**20)

    def pick(kernel, count, source, name):
        return pl.pallas_call(
            kernel,
            out_shape=pltpu.VMEM((count, BS, BS), jnp.bfloat16),
            in_specs=[HBM],
            out_specs=VMEM,
            scratch_shapes=[pltpu.SemaphoreType.DMA((count,))],
            compiler_params=small,
            name=name,
        )(pltpu.with_memory_space_constraint(source, pltpu.HBM))

    picked = pick(pick_kernel, SHARE, density, "pick")
    density, picked = lax.optimization_barrier((density, picked))
    inner = lax.ppermute(density, "grid", inner_pairs)
    near = lax.ppermute(picked, "grid", outer_pairs)
    far = lax.ppermute(pick(pick_far_kernel, FAR * LISTED, density, "pick_far"), "grid", outer_pairs)

    listed, place = tables(pattern)
    store_shape = shape(STORE, BS, BS)
    out_shape = shape(ROWS, BS, 2 * BS, dtype=jnp.float32)

    def working(rows):
        return [
            pltpu.VMEM((rows, BS, SPAN), jnp.float32),
            pltpu.VMEM((rows, BS, SPAN), jnp.bfloat16),
            pltpu.VMEM((rows, BS, 2 * BS), jnp.float32),
            pltpu.SMEM((ROWS * LISTED,), jnp.int32),
            pltpu.SemaphoreType.DMA((2,)),
            pltpu.SemaphoreType.DMA((rows,)),
        ]

    half_shape = shape(ROWS // 2, BS, SPAN, dtype=jnp.float32)
    store, partial = pl.pallas_call(
        close_kernel,
        out_shape=(store_shape, half_shape),
        in_specs=[SMEM, SMEM, VMEM, VMEM],
        out_specs=(VMEM, VMEM),
        compiler_params=limits,
        cost_estimate=cost(2_000_000_000),
        name="close",
    )(listed, place, density, inner)
    near, partial = lax.optimization_barrier((near, partial))
    swapped = lax.ppermute(near, ("layer", "grid"), swap_pairs)
    partial2 = pl.pallas_call(
        close_kernel2,
        out_shape=half_shape,
        in_specs=[SMEM, SMEM, VMEM, VMEM],
        out_specs=VMEM,
        compiler_params=limits,
        cost_estimate=cost(2_000_000_000),
        name="close2",
    )(listed, place, density, store)
    store, sums = pl.pallas_call(
        near_kernel,
        out_shape=(store_shape, shape(ROWS, BS, SPAN, dtype=jnp.float32)),
        in_specs=[SMEM, SMEM] + [VMEM] * 5,
        out_specs=(VMEM, VMEM),
        scratch_shapes=[pltpu.SMEM((ROWS * LISTED,), jnp.int32), pltpu.SemaphoreType.DMA((1,))],
        input_output_aliases={6: 0},
        compiler_params=limits,
        cost_estimate=cost(2_000_000_000),
        name="near",
    )(listed, place, density, near, partial, partial2, store)
    store, rest, out = pl.pallas_call(
        swapped_kernel,
        out_shape=(store_shape, shape(FAR, BS, SPAN, dtype=jnp.float32), out_shape),
        in_specs=[SMEM, SMEM] + [VMEM] * 4,
        out_specs=(VMEM, VMEM, ANY),
        scratch_shapes=working(NEAR),
        input_output_aliases={5: 0},
        compiler_params=limits,
        cost_estimate=cost(2_000_000_000),
        name="swapped",
    )(listed, place, density, swapped, sums, store)
    return pl.pallas_call(
        far_kernel,
        out_shape=(store_shape, out_shape),
        in_specs=[SMEM, SMEM] + [VMEM] * 4 + [ANY],
        out_specs=(VMEM, ANY),
        scratch_shapes=working(FAR),
        input_output_aliases={5: 0, 6: 1},
        compiler_params=limits,
        cost_estimate=cost(2_000_000_000),
        name="far",
    )(listed, place, density, far, rest, store, out)[1]


def solution(mesh):
    placed = (P("grid", None, None), P())
    return jax.shard_map(
        local, mesh=mesh, in_specs=placed, out_specs=P("grid", None, "layer"), check_vma=False
    )
```

time: 280 us -> 33.7 us (0.12); the launches traced: 277 us -> 33.3 us
  waiting for transfers between devices: 119 us -> 3.74 us
  blocking collectives: 71.5 us -> 0 us
  local copies, waits for them, and re-layouts: 47.8 us -> 0.48 us
  Pallas kernels: 0 us -> 19 us
  between operations: 14.2 us -> 0.13 us
  matrix products: 12.9 us -> 0 us
  other arithmetic: 3.91 us -> 0.23 us
    unnamed x2 -> x0, waiting for transfers between devices: 101 us -> none
    unnamed x1 -> x0, blocking collectives: 71.5 us -> none
    gather x9 -> x0, local copies, waits for them, and re-layouts: 28 us -> none  [the longest x8 27.4 us: align_row(): fetched = jnp.take(padded_blocks, row_places, axis=0)]
    pallas_call x0 -> x7, Pallas kernels: none -> 19 us  [the longest x2 4.54 us: pick(): pl.pallas_call(kernel, out_shape=pltpu.VMEM((count, BS, BS), jnp.bfloat16...]
    ppermute x2 -> x4, waiting for transfers between devices: 17.4 us -> 3.74 us  [the longest x1 3.38 us: local(): swapped = lax.ppermute(near, ('layer', 'grid'), swap_pairs)]
    dot_general x10 -> x0, matrix products: 12.9 us -> none  [the longest x1 5.07 us: local(): jnp.einsum('ixay,iayjz->ixjz', left_slots, aligned, preferred_element_typ...]
    unnamed x12 -> x8, local copies, waits for them, and re-layouts: 10.3 us -> 0.02 us
    dynamic_update_slice x8 -> x0, local copies, waits for them, and re-layouts: 7.35 us -> none  [local(): aligned = lax.map(align_row, (located, selector))]
  transfers between devices with their start and end apart: 3 -> 4, of which waited for: 2 -> 2; matrix products, arithmetic and copies ran while one was open for 2% -> 2% of each run, Pallas kernels for 0% -> 43%
where the time goes in v3:
time: 33.7 us; the launch traced here: 33.3 us
  Pallas kernels  19 us (56%)
  starting transfers between devices  9.72 us (29%)
  waiting for transfers between devices  3.74 us (11%)
  local copies, waits for them, and re-layouts  0.48 us (1%)
    ppermute x1, starting transfers between devices, local(): near = lax.ppermute(picked, 'grid', outer_pairs)  8.15 us
    pallas_call x2, Pallas kernels, pick(): pl.pallas_call(kernel, out_shape=pltpu.VMEM((count, BS, BS), jnp.bfloat16...  4.54 us
    pallas_call x1, Pallas kernels, local(): pl.pallas_call(close_kernel, out_shape=(store_shape, half_shape), in_spec...  4.15 us
    ppermute x1, waiting for transfers between devices, local(): swapped = lax.ppermute(near, ('layer', 'grid'), swap_pairs)  3.38 us
    pallas_call x1, Pallas kernels, local(): pl.pallas_call(swapped_kernel, out_shape=(store_shape, shape(FAR, BS, SPA...  2.96 us
    pallas_call x1, Pallas kernels, local(): pl.pallas_call(far_kernel, out_shape=(store_shape, out_shape), in_specs=[...  2.66 us
    pallas_call x1, Pallas kernels, local(): pl.pallas_call(close_kernel2, out_shape=half_shape, in_specs=[SMEM, SMEM,...  2.4 us
    pallas_call x1, Pallas kernels, local(): pl.pallas_call(near_kernel, out_shape=(store_shape, shape(ROWS, BS, SPAN,...  2.32 us
  transfers between devices with their start and end apart: 4, of which 2 were waited for; matrix products, arithmetic and copies ran while one was open for 2% of the time, Pallas kernels for 43%

profile of v3, /device:TPU:16, one launch (start us, length us, event | category | flops | bytes accessed | tf_op | source)
XLA Modules:
  0.0 33.3 jit_solution(385267848444614071)
XLA Ops:
  0.0 0.0 copy-start.2
  0.0 0.0 copy-start.3
  0.0 0.0 copy-start
  0.0 0.0 copy-start.1
  0.0 2.1 %pick.1 = bf16[16,128,128]{2,1,0:T(8,128)(2,1)} custom-call(bf16[8,128,1024]{2,1,0:T(8,128)(2,1)} %own.4), custom_call_target="tpu_custom_call" | custom-call | tf_op jit(solution)/shard_map/pick/pallas_call | solution.py:290
  2.1 0.1 collective-permute-start.2
  2.2 8.1 %collective-permute-start.1 = (bf16[16,128,128]{2,1,0:T(8,128)(2,1)}, bf16[16,128,128]{2,1,0:T(8,128)(2,1)}, u32[]{:S(2)}, u32[]{:S(2)}) collective-permute-start(bf16[16,128,128]{2,1,0:T(8,128)(2,1)} %pick.1), channel_id=1, source_target_pairs={{0,63},{1,2},{2,1},{3,4},{4,3},{5,6},{6,5},{7,8},{8,7},{9,10},{10,... | collective-permute-start | bytes 1572872 | tf_op jit(solution)/shard_map/ppermute | solution.py:303
  10.4 2.4 %pick_far.1 = bf16[32,128,128]{2,1,0:T(8,128)(2,1)} custom-call(bf16[8,128,1024]{2,1,0:T(8,128)(2,1)} %own.4), custom_call_target="tpu_custom_call" | custom-call | tf_op jit(solution)/shard_map/pick_far/pallas_call | solution.py:290
  12.8 0.1 collective-permute-start
  12.9 0.0 copy-done.1
  13.0 0.1 fusion.11
  13.0 0.1 compare_select_fusion
  13.1 0.1 rev.3
  13.2 0.0 copy-done.2
  13.2 0.0 copy-done.3
  13.2 0.1 slice.59
  13.3 0.1 select_select_fusion
  13.4 0.1 reshape.45.place
  13.5 0.1 copy.10
  13.6 0.1 reshape.40.listed
  13.7 0.0 collective-permute-done.2.inner
  13.7 0.0 copy-done
  13.7 4.1 %close.1 = (bf16[193,128,128]{2,1,0:T(8,128)(2,1)S(1)}, f32[4,128,1024]{2,1,0:T(8,128)S(1)}) custom-call(s32[64]{0:T(128)S(1)} %reshape.40.listed, s32[600]{0:T(1024)S(1)} %reshape.45.place, bf16[8,128,1024]{2,1,0:T(8,128)(2,1)S(1)} %copy-done, bf16[8,128,1024]{2,1,0:T(8,128)(2,1)} %collective-permute-done.2.inner), custom_call_target="tpu_custom_call" | custom-call | flops 2000000000 | bytes 4000000 | tf_op jit(solution)/shard_map/close/pallas_call | solution.py:321
  17.8 0.0 collective-permute-done.1.near
  17.9 1.4 %collective-permute-start.3 = (bf16[16,128,128]{2,1,0:T(8,128)(2,1)}, bf16[16,128,128]{2,1,0:T(8,128)(2,1)S(1)}, u32[]{:S(2)}, u32[]{:S(2)}) collective-permute-start(bf16[16,128,128]{2,1,0:T(8,128)(2,1)} %collective-permute-done.1.near), channel_id=1, source_target_pairs={{0,64},{1,193},{2,66},{3,195},{4,68},{5,197},{6,70},{7,199},{8,72}... | collective-permute-start | bytes 1572872 | tf_op jit(solution)/shard_map/ppermute | solution.py:331
  19.2 2.4 %close2.1.partial2 = f32[4,128,1024]{2,1,0:T(8,128)S(1)} custom-call(s32[64]{0:T(128)S(1)} %reshape.40.listed, s32[600]{0:T(1024)S(1)} %reshape.45.place, bf16[8,128,1024]{2,1,0:T(8,128)(2,1)S(1)} %copy-done, bf16[193,128,128]{2,1,0:T(8,128)(2,1)S(1)} %get-tuple-element.22.store._), custom_call_target="tpu_custom_call" | custom-call | flops 2000000000 | bytes 4000000 | tf_op jit(solution)/shard_map/close2/pallas_call | solution.py:332
  21.6 2.3 %near.1 = (bf16[193,128,128]{2,1,0:T(8,128)(2,1)S(1)}, f32[8,128,1024]{2,1,0:T(8,128)S(1)}) custom-call(s32[64]{0:T(128)S(1)} %reshape.40.listed, s32[600]{0:T(1024)S(1)} %reshape.45.place, bf16[8,128,1024]{2,1,0:T(8,128)(2,1)S(1)} %copy-done, bf16[16,128,128]{2,1,0:T(8,128)(2,1)} %collective-permute-done.1.near, ...), custom_call_target="tpu_custom_call", output_to_operand_aliasing={{0}: (6, {})} | custom-call | flops 2000000000 | bytes 4000000 | tf_op jit(solution)/shard_map/near/pallas_call | solution.py:341
  24.0 3.4 %collective-permute-done.3.swapped = bf16[16,128,128]{2,1,0:T(8,128)(2,1)S(1)} collective-permute-done((bf16[16,128,128]{2,1,0:T(8,128)(2,1)}, bf16[16,128,128]{2,1,0:T(8,128)(2,1)S(1)}, u32[]{:S(2)}, u32[]{:S(2)}) %collective-permute-start.3) | collective-permute-done | bytes 524320 | tf_op jit(solution)/shard_map/ppermute | solution.py:331
  27.3 3.0 %swapped.1 = (bf16[193,128,128]{2,1,0:T(8,128)(2,1)S(1)}, f32[4,128,1024]{2,1,0:T(8,128)S(1)}, f32[8,128,256]{2,1,0:T(8,128)}) custom-call(s32[64]{0:T(128)S(1)} %reshape.40.listed, s32[600]{0:T(1024)S(1)} %reshape.45.place, bf16[8,128,1024]{2,1,0:T(8,128)(2,1)S(1)} %copy-done, ...), custom_call_target="tpu_custom_call", output_to_operand_aliasing={{0}: (5, {})} | custom-call | flops 2000000000 | bytes 4000000 | tf_op jit(solution)/shard_map/swapped/pallas_call | solution.py:352
  30.3 0.4 %collective-permute-done.far = bf16[32,128,128]{2,1,0:T(8,128)(2,1)S(1)} collective-permute-done((bf16[32,128,128]{2,1,0:T(8,128)(2,1)}, bf16[32,128,128]{2,1,0:T(8,128)(2,1)S(1)}, u32[]{:S(2)}, u32[]{:S(2)}) %collective-permute-start) | collective-permute-done | bytes 1048608 | tf_op jit(solution)/shard_map/ppermute | solution.py:304
  30.7 2.7 %far.1 = (bf16[193,128,128]{2,1,0:T(8,128)(2,1)S(1)}, f32[8,128,256]{2,1,0:T(8,128)}) custom-call(s32[64]{0:T(128)S(1)} %reshape.40.listed, s32[600]{0:T(1024)S(1)} %reshape.45.place, bf16[8,128,1024]{2,1,0:T(8,128)(2,1)S(1)} %copy-done, bf16[32,128,128]{2,1,0:T(8,128)(2,1)S(1)} %collective-permute-done.far, ...), custom_call_target="tpu_custom_call", output_to_operand_aliasing={{0}: (5, {}), {1}: (6, {})} | custom-call | flops 2000000000 | bytes 4000000 | tf_op jit(solution)/shard_map/far/pallas_call | solution.py:363
  (3 shorter events, 0.0 us)
Async XLA Ops:
  0.0 13.2 %copy-start.2 = (s32[25,8]{0,1:T(8,128)S(1)}, s32[25,8]{0,1:T(8,128)}, u32[]{:S(2)}) copy-start(s32[25,8]{0,1:T(8,128)} %constant.40.clone) | copy-start | bytes 2404
  0.0 13.2 %copy-start.3 = (s32[25,8]{0,1:T(8,128)S(1)}, s32[25,8]{0,1:T(8,128)}, u32[]{:S(2)}) copy-start(s32[25,8]{0,1:T(8,128)} %constant.41.clone) | copy-start | bytes 2404
  0.0 13.7 %copy-start = (bf16[8,128,1024]{2,1,0:T(8,128)(2,1)S(1)}, bf16[8,128,1024]{2,1,0:T(8,128)(2,1)}, u32[]{:S(2)}) copy-start(bf16[8,128,1024]{2,1,0:T(8,128)(2,1)} %own.4) | copy-start | bytes 6291460
  0.0 12.9 %copy-start.1 = (s32[512,8]{0,1:T(8,128)S(1)}, s32[512,8]{0,1:T(8,128)}, u32[]{:S(2)}) copy-start(s32[512,8]{0,1:T(8,128)} %param.5) | copy-start | bytes 49156
  2.1 11.6 %collective-permute-start.2 = (bf16[8,128,1024]{2,1,0:T(8,128)(2,1)}, bf16[8,128,1024]{2,1,0:T(8,128)(2,1)}, u32[]{:S(2)}, u32[]{:S(2)}) collective-permute-start(bf16[8,128,1024]{2,1,0:T(8,128)(2,1)} %own.4), channel_id=1, source_target_pairs={{0,1},{1,0},{2,3},{3,2},{4,5},{5,4},{6,7},{7,6},{8,9},{9,8},{10,11... | collective-permute-start | bytes 6291464 | tf_op jit(solution)/shard_map/ppermute | solution.py:302
  2.2 15.6 %collective-permute-start.1 = (bf16[16,128,128]{2,1,0:T(8,128)(2,1)}, bf16[16,128,128]{2,1,0:T(8,128)(2,1)}, u32[]{:S(2)}, u32[]{:S(2)}) collective-permute-start(bf16[16,128,128]{2,1,0:T(8,128)(2,1)} %pick.1), channel_id=1, source_target_pairs={{0,63},{1,2},{2,1},{3,4},{4,3},{5,6},{6,5},{7,8},{8,7},{9,10},{10,... | collective-permute-start | bytes 1572872 | tf_op jit(solution)/shard_map/ppermute | solution.py:303
  12.8 17.8 %collective-permute-start = (bf16[32,128,128]{2,1,0:T(8,128)(2,1)}, bf16[32,128,128]{2,1,0:T(8,128)(2,1)S(1)}, u32[]{:S(2)}, u32[]{:S(2)}) collective-permute-start(bf16[32,128,128]{2,1,0:T(8,128)(2,1)} %pick_far.1), channel_id=1, source_target_pairs={{0,63},{1,2},{2,1},{3,4},{4,3},{5,6},{6,5},{7,8},{8,7},{9,10},{10,... | collective-permute-start | bytes 3145736 | tf_op jit(solution)/shard_map/ppermute | solution.py:304
  17.9 9.5 %collective-permute-start.3 = (bf16[16,128,128]{2,1,0:T(8,128)(2,1)}, bf16[16,128,128]{2,1,0:T(8,128)(2,1)S(1)}, u32[]{:S(2)}, u32[]{:S(2)}) collective-permute-start(bf16[16,128,128]{2,1,0:T(8,128)(2,1)} %collective-permute-done.1.near), channel_id=1, source_target_pairs={{0,64},{1,193},{2,66},{3,195},{4,68},{5,197},{6,70},{7,199},{8,72}... | collective-permute-start | bytes 1572872 | tf_op jit(solution)/shard_map/ppermute | solution.py:331

commit v4 on v3

--- a/solution.py
+++ b/solution.py
@@ -11,13 +11,17 @@
 BS = 128
 SPAN = LISTED * BS
 WINDOW = 3 * ROWS
-FAR = 4
+FAR = 5
 NEAR = ROWS - FAR
 SHARE = NEAR * LISTED // 2
+FAR_BLOCKS = FAR * LISTED
+FIRST = 28
+REST = FAR_BLOCKS - FIRST
+EARLY_EVERY = 16
 INNER_AT = ROWS * LISTED
 NEAR_AT = 2 * ROWS * LISTED
-FAR_AT = NEAR_AT + NEAR * LISTED
-ZERO = FAR_AT + FAR * LISTED
+FAR_AT = NEAR_AT + 2 * SHARE
+ZERO = FAR_AT + FAR_BLOCKS
 STORE = ZERO + 1
 
 ANY = pl.BlockSpec(memory_space=pl.ANY)
@@ -27,11 +31,12 @@
 
 
 def places(odd):
-    rows = []
-    for w in range(FAR):
-        rows.append([FAR_AT + w * LISTED + s for s in range(LISTED)])
-    for w in range(FAR, ROWS):
-        rows.append([NEAR_AT + (w - FAR) * LISTED + s for s in range(LISTED)])
+    middle = LISTED // 2
+    rows = [
+        [NEAR_AT + s for s in range(LISTED)],
+        [NEAR_AT + LISTED + s + (SHARE - middle if s >= middle else 0) for s in range(LISTED)],
+        [NEAR_AT + SHARE + s for s in range(LISTED)],
+    ]
     for base in (0, INNER_AT):
         for e in range(ROWS):
             i = ROWS - 1 - e if odd else e
@@ -40,7 +45,7 @@
     return np.array(rows, np.int32)
 
 
-def tables(pattern):
+def tables(pattern, far_places):
     blocks = pattern.shape[0]
     g = lax.axis_index("grid")
     odd = g % 2 == 1
@@ -53,6 +58,7 @@
     listed = columns[ROWS : 2 * ROWS]
     columns = jnp.concatenate([columns, jnp.full((1, LISTED), -1, jnp.int32)], axis=0)
     at = jnp.where(odd, places(True), places(False))
+    at = jnp.concatenate([far_places.reshape(FAR, LISTED), at], axis=0)
     xs = lax.broadcasted_iota(jnp.int32, (WINDOW + 1, WINDOW), 1)
     place = jnp.full((WINDOW + 1, WINDOW), ZERO, jnp.int32)
     for s in range(LISTED):
@@ -60,6 +66,50 @@
     return listed.reshape(-1), place.reshape(-1)
 
 
+def ones(bits):
+    bits = (bits & 0x55555555) + ((bits >> 1) & 0x55555555)
+    bits = (bits & 0x33333333) + ((bits >> 2) & 0x33333333)
+    bits = (bits & 0x0F0F0F0F) + ((bits >> 4) & 0x0F0F0F0F)
+    bits = bits + (bits >> 8)
+    return (bits + (bits >> 16)) & 0xFF
+
+
+def positions(pattern):
+    blocks = pattern.shape[1]
+    row = lax.broadcasted_iota(jnp.int32, pattern.shape, 1)
+    slot = lax.broadcasted_iota(jnp.int32, pattern.shape, 0)
+    offset = pattern - row + ROWS
+    offset = jnp.where(offset < 0, offset + blocks, offset)
+    offset = jnp.where(offset >= blocks, offset - blocks, offset)
+    bits = jnp.sum(jnp.left_shift(1, offset), axis=0, keepdims=True)
+    bits = jnp.broadcast_to(bits, pattern.shape)
+    k = row & (ROWS - 1)
+    forward = (row & ROWS) != 0
+    uses = jnp.zeros(pattern.shape, jnp.int32)
+    for d in range(1, ROWS + 1):
+        after = pltpu.roll(bits, blocks - d, 1)
+        before = pltpu.roll(bits, d, 1)
+        hit_after = jnp.logical_and(k + d >= ROWS, ((after >> (ROWS - d)) & 1) == 1)
+        hit_before = jnp.logical_and(k - d < 0, ((before >> (ROWS + d)) & 1) == 1)
+        uses = uses | jnp.where(
+            forward, jnp.where(hit_after, after << d, 0), jnp.where(hit_before, before >> d, 0)
+        )
+    far = jnp.where(forward, k, ROWS - 1 - k) < FAR
+    mask = jnp.where(far, bits & uses, 0)
+    sent = (mask >> offset) & 1
+    up_to = sent
+    for d in (1, 2, 4):
+        up_to = up_to + jnp.where(slot >= d, pltpu.roll(up_to, d, 0), 0)
+    count = ones(mask)
+    ahead, behind = count, count
+    for d in (1, 2, 4):
+        ahead = ahead + jnp.where(k >= d, pltpu.roll(ahead, d, 1), 0)
+        behind = behind + jnp.where(k < ROWS - d, pltpu.roll(behind, blocks - d, 1), 0)
+    position = jnp.where(forward, ahead, behind) - count + up_to - sent
+    most = jnp.max(ahead.astype(jnp.float32))
+    return jnp.where(sent == 1, position, FAR_BLOCKS), most
+
+
 def parity():
     return lax.rem(lax.axis_index("grid"), 2)
 
@@ -76,27 +126,73 @@
     return jnp.where(parity() == 1, w, ROWS - 1 - w)
 
 
-def pick_kernel(source, out, sems):
-    copies = []
-    for n in range(SHARE):
-        row = sent_row(FAR + (NEAR // 2) * half() + n // LISTED)
-        block = source.at[row, :, pl.ds(n % LISTED * BS, BS)]
-        copies.append(pltpu.make_async_copy(block, out.at[n], sems.at[n]))
+def pick_kernel(source, pattern, out, moves, flag, listed, sems):
+    whole = sent_row(FAR + 2 * half())
+    start = pl.multiple_of(half() * (SPAN // 2), SPAN // 2)
+    copies = [
+        pltpu.make_async_copy(pattern, listed, sems.at[0]),
+        pltpu.make_async_copy(source.at[whole], out.at[:, pl.ds(0, SPAN)], sems.at[1]),
+        pltpu.make_async_copy(
+            source.at[sent_row(FAR + 1), :, pl.ds(start, SPAN // 2)], out.at[:, pl.ds(SPAN, SPAN // 2)], sems.at[2]
+        ),
+    ]
     for copy in copies:
         copy.start()
-    for copy in copies:
+    copies[0].wait()
+    position, most = positions(listed[...])
+    blocks = pattern.shape[1]
+    shift = blocks - ROWS * lax.rem(lax.axis_index("grid") + lax.axis_size("grid") - 1, lax.axis_size("grid"))
+    moves[...] = pltpu.roll(position, lax.rem(shift, blocks), 1)[:, :BS]
+    flag[0] = (most > FIRST).astype(jnp.int32)
+    for copy in copies[1:]:
         copy.wait()
 
 
-def pick_far_kernel(source, out, sems):
-    copies = []
-    for n in range(FAR * LISTED):
-        block = source.at[sent_row(n // LISTED), :, pl.ds(n % LISTED * BS, BS)]
-        copies.append(pltpu.make_async_copy(block, out.at[n], sems.at[n]))
-    for copy in copies:
-        copy.start()
-    for copy in copies:
-        copy.wait()
+def waits_long():
+    return lax.rem(lax.axis_index("grid"), EARLY_EVERY) == 0
+
+
+def pack(moves, source, own, packed, sems):
+    start = jnp.where(parity() == 1, 0, ROWS - FAR)
+    rows = pltpu.make_async_copy(source.at[pl.ds(start, FAR)], own, sems.at[1])
+    rows.start()
+    rows.wait()
+    for k in range(FAR):
+        held = jnp.where(parity() == 1, k, FAR - 1 - k)
+        for s in range(LISTED):
+            packed[moves[s, ROWS + sent_row(k)]] = own[held, :, s * BS : (s + 1) * BS]
+
+
+def pack_first(moves, source, first, own, packed, sems):
+    pack(moves, source, own, packed, sems)
+    copy = pltpu.make_async_copy(packed.at[pl.ds(0, FIRST)], first, sems.at[0])
+    copy.start()
+    copy.wait()
+
+
+def early_pack_kernel(moves, source, first, unused, *scratch):
+    @pl.when(waits_long())
+    def _():
+        pack_first(moves, source, first, *scratch)
+
+
+def late_pack_kernel(moves, source, _, first, far_places, *scratch):
+    for k in range(FAR):
+        row = jnp.where(parity() == 0, k, WINDOW - 1 - k)
+        for s in range(LISTED):
+            place = moves[s, row]
+            far_places[k * LISTED + s] = jnp.where(place == FAR_BLOCKS, ZERO, FAR_AT + place)
+
+    @pl.when(jnp.logical_not(waits_long()))
+    def _():
+        pack_first(moves, source, first, *scratch)
+
+
+def pack_rest_kernel(moves, source, rest, own, packed, sems):
+    pack(moves, source, own, packed, sems)
+    copy = pltpu.make_async_copy(packed.at[pl.ds(FIRST, REST)], rest, sems.at[0])
+    copy.start()
+    copy.wait()
 
 
 class Blocks:
@@ -123,35 +219,30 @@
         return total
 
 
-def close_rows(listed, place, own, store, partial, first):
-    def one_row(n, carry):
-        e = first + n
+def close_kernel(listed, place, own, inner, near, store, partial):
+    for n, source in enumerate((own, inner)):
+        for r in range(ROWS):
+            for s in range(LISTED):
+                store[n * INNER_AT + s * ROWS + r] = source[r, :, s * BS : (s + 1) * BS]
+    place_share(near, store, True)
+    store[ZERO] = jnp.zeros((BS, BS), jnp.bfloat16)
+    whole = FAR + 2 * half()
+
+    def one_row(e, carry):
         blocks = Blocks(listed, place, store, e)
         i = row_of(e)
         rows = []
         for c in range(LISTED):
             row = blocks.row(c)
-            rows.append(jnp.where(row < ROWS, WINDOW, row))
+            away = jnp.logical_and(row < ROWS, row != whole)
+            rows.append(jnp.where(away, WINDOW, row))
         for a in range(0, LISTED, 2):
-            partial[n, :, a * BS : (a + 2) * BS] = blocks.times(
+            partial[e, :, a * BS : (a + 2) * BS] = blocks.times(
                 lambda c: own[i, :, c * BS : (c + 2) * BS], rows, a
             )
         return carry
 
-    lax.fori_loop(0, ROWS // 2, one_row, 0)
-
-
-def close_kernel(listed, place, own, inner, store, partial):
-    for n, source in enumerate((own, inner)):
-        for r in range(ROWS):
-            for s in range(LISTED):
-                store[n * INNER_AT + s * ROWS + r] = source[r, :, s * BS : (s + 1) * BS]
-    store[ZERO] = jnp.zeros((BS, BS), jnp.bfloat16)
-    close_rows(listed, place, own, store, partial, 0)
-
-
-def close_kernel2(listed, place, own, store, partial):
-    close_rows(listed, place, own, store, partial, ROWS // 2)
+    lax.fori_loop(0, ROWS, one_row, 0)
 
 
 def chosen(blocks, low, high, index, most):
@@ -230,24 +321,17 @@
         copy.wait()
 
 
-def share_low(mine):
-    return FAR + NEAR // 2 * (half() if mine else 1 - half())
-
-
-def near_kernel(listed, place, own, near, partial, partial2, _, store, sums, index, sems):
-    insert([(near, NEAR_AT + SHARE * half(), SHARE)], store, sems)
-    low = share_low(True)
-    source = lambda e: partial.at[e] if e < ROWS // 2 else partial2.at[e - ROWS // 2]
-    add_rows(
-        listed, place, store, own, source, sums, list(range(ROWS)), low, low + 2, [2] * ROWS, index
-    )
+def place_share(share, store, mine):
+    base = NEAR_AT + SHARE * (half() if mine else 1 - half())
+    for n in range(SHARE):
+        store[base + n] = share[:, n * BS : (n + 1) * BS]
 
 
 def swapped_kernel(
-    listed, place, own, swapped, sums, _, store, rest, out, total, square, result, index, sems, out_sems
+    listed, place, own, swapped, sums, _, store, rest, out, total, square, result, index, out_sems
 ):
-    insert([(swapped, NEAR_AT + SHARE * (1 - half()), SHARE)], store, sems)
-    low = share_low(False)
+    place_share(swapped, store, False)
+    low = FAR + 1 - half()
     source = lambda e: sums.at[e]
     ended, left = list(range(FAR, ROWS)), list(range(FAR))
     add_rows(listed, place, store, own, source, total, ended, low, low + 2, [2] * NEAR, index)
@@ -256,12 +340,12 @@
 
 
 def far_kernel(
-    listed, place, own, far, rest, _s, _o, store, out, total, square, result, index, sems, out_sems
+    listed, place, own, first, last, rest, _s, _o, store, out, total, square, result, index, out_sems, sems
 ):
-    insert([(far, FAR_AT, FAR * LISTED)], store, sems)
+    insert([(first, FAR_AT, FIRST), (last, FAR_AT + FIRST, REST)], store, sems)
     source = lambda e: rest.at[e]
     rows = list(range(FAR))
-    add_rows(listed, place, store, own, source, total, rows, 0, FAR, [4, 4, 2, 2], index)
+    add_rows(listed, place, store, own, source, total, rows, 0, FAR, [6, 4, 4, 2, 2], index)
     finish(listed, place, store, total, rows, square, result, out, out_sems)
 
 
@@ -286,24 +370,67 @@
     small = pltpu.CompilerParams(vmem_limit_bytes=8 * 2**20)
     limits = pltpu.CompilerParams(vmem_limit_bytes=24 * 2**20)
 
-    def pick(kernel, count, source, name):
-        return pl.pallas_call(
-            kernel,
-            out_shape=pltpu.VMEM((count, BS, BS), jnp.bfloat16),
-            in_specs=[HBM],
-            out_specs=VMEM,
-            scratch_shapes=[pltpu.SemaphoreType.DMA((count,))],
-            compiler_params=small,
-            name=name,
-        )(pltpu.with_memory_space_constraint(source, pltpu.HBM))
-
-    picked = pick(pick_kernel, SHARE, density, "pick")
-    density, picked = lax.optimization_barrier((density, picked))
-    inner = lax.ppermute(density, "grid", inner_pairs)
+    in_hbm = pltpu.with_memory_space_constraint(density, pltpu.HBM)
+    by_slot = pltpu.with_memory_space_constraint(pattern.T, pltpu.HBM)
+    picked, moves, flag = pl.pallas_call(
+        pick_kernel,
+        out_shape=(
+            shape(BS, SHARE * BS),
+            jax.ShapeDtypeStruct((LISTED, BS), jnp.int32),
+            jax.ShapeDtypeStruct((1,), jnp.int32),
+        ),
+        in_specs=[HBM, HBM],
+        out_specs=(VMEM, VMEM, SMEM),
+        scratch_shapes=[pltpu.VMEM(by_slot.shape, jnp.int32), pltpu.SemaphoreType.DMA((3,))],
+        compiler_params=small,
+        name="pick",
+    )(in_hbm, by_slot)
+    inner_sent, picked = lax.optimization_barrier((density, picked))
+    inner = lax.ppermute(inner_sent, "grid", inner_pairs)
+    packing = dict(
+        scratch_shapes=[
+            pltpu.VMEM((FAR, BS, SPAN), jnp.bfloat16),
+            pltpu.VMEM((FAR_BLOCKS + 1, BS, BS), jnp.bfloat16),
+            pltpu.SemaphoreType.DMA((2,)),
+        ],
+        compiler_params=small,
+    )
+    first, unused = pl.pallas_call(
+        early_pack_kernel,
+        out_shape=(shape(FIRST, BS, BS), shape(REST, BS, BS)),
+        in_specs=[SMEM, HBM],
+        out_specs=(ANY, ANY),
+        name="early_pack",
+        **packing,
+    )(moves, in_hbm)
+    picked, first = lax.optimization_barrier((picked, first))
     near = lax.ppermute(picked, "grid", outer_pairs)
-    far = lax.ppermute(pick(pick_far_kernel, FAR * LISTED, density, "pick_far"), "grid", outer_pairs)
-
-    listed, place = tables(pattern)
+    first, far_places = pl.pallas_call(
+        late_pack_kernel,
+        out_shape=(shape(FIRST, BS, BS), jax.ShapeDtypeStruct((FAR_BLOCKS,), jnp.int32)),
+        in_specs=[SMEM, HBM, ANY],
+        out_specs=(ANY, SMEM),
+        input_output_aliases={2: 0},
+        name="late_pack",
+        **packing,
+    )(moves, in_hbm, first)
+    first = lax.ppermute(first, "grid", outer_pairs)
+
+    def send_rest(_):
+        rest = pl.pallas_call(
+            pack_rest_kernel,
+            out_shape=shape(REST, BS, BS),
+            in_specs=[SMEM, HBM],
+            out_specs=ANY,
+            name="pack_rest",
+            **packing,
+        )(moves, in_hbm)
+        return lax.ppermute(rest, "grid", outer_pairs)
+
+    last = lax.cond(flag[0] > 0, send_rest, lambda blocks: blocks, unused)
+
+    listed, place = tables(pattern, far_places)
+    listed, last = lax.optimization_barrier((listed, last))
     store_shape = shape(STORE, BS, BS)
     out_shape = shape(ROWS, BS, 2 * BS, dtype=jnp.float32)
 
@@ -313,42 +440,19 @@
             pltpu.VMEM((rows, BS, SPAN), jnp.bfloat16),
             pltpu.VMEM((rows, BS, 2 * BS), jnp.float32),
             pltpu.SMEM((ROWS * LISTED,), jnp.int32),
-            pltpu.SemaphoreType.DMA((2,)),
             pltpu.SemaphoreType.DMA((rows,)),
         ]
 
-    half_shape = shape(ROWS // 2, BS, SPAN, dtype=jnp.float32)
-    store, partial = pl.pallas_call(
+    swapped = lax.ppermute(near, ("layer", "grid"), swap_pairs)
+    store, sums = pl.pallas_call(
         close_kernel,
-        out_shape=(store_shape, half_shape),
-        in_specs=[SMEM, SMEM, VMEM, VMEM],
+        out_shape=(store_shape, shape(ROWS, BS, SPAN, dtype=jnp.float32)),
+        in_specs=[SMEM, SMEM, VMEM, VMEM, VMEM],
         out_specs=(VMEM, VMEM),
         compiler_params=limits,
-        cost_estimate=cost(2_000_000_000),
+        cost_estimate=cost(4_000_000_000),
         name="close",
-    )(listed, place, density, inner)
-    near, partial = lax.optimization_barrier((near, partial))
-    swapped = lax.ppermute(near, ("layer", "grid"), swap_pairs)
-    partial2 = pl.pallas_call(
-        close_kernel2,
-        out_shape=half_shape,
-        in_specs=[SMEM, SMEM, VMEM, VMEM],
-        out_specs=VMEM,
-        compiler_params=limits,
-        cost_estimate=cost(2_000_000_000),
-        name="close2",
-    )(listed, place, density, store)
-    store, sums = pl.pallas_call(
-        near_kernel,
-        out_shape=(store_shape, shape(ROWS, BS, SPAN, dtype=jnp.float32)),
-        in_specs=[SMEM, SMEM] + [VMEM] * 5,
-        out_specs=(VMEM, VMEM),
-        scratch_shapes=[pltpu.SMEM((ROWS * LISTED,), jnp.int32), pltpu.SemaphoreType.DMA((1,))],
-        input_output_aliases={6: 0},
-        compiler_params=limits,
-        cost_estimate=cost(2_000_000_000),
-        name="near",
-    )(listed, place, density, near, partial, partial2, store)
+    )(listed, place, density, inner, near)
     store, rest, out = pl.pallas_call(
         swapped_kernel,
         out_shape=(store_shape, shape(FAR, BS, SPAN, dtype=jnp.float32), out_shape),
@@ -363,14 +467,14 @@
     return pl.pallas_call(
         far_kernel,
         out_shape=(store_shape, out_shape),
-        in_specs=[SMEM, SMEM] + [VMEM] * 4 + [ANY],
+        in_specs=[SMEM, SMEM] + [VMEM] * 5 + [ANY],
         out_specs=(VMEM, ANY),
-        scratch_shapes=working(FAR),
-        input_output_aliases={5: 0, 6: 1},
+        scratch_shapes=working(FAR) + [pltpu.SemaphoreType.DMA((2,))],
+        input_output_aliases={6: 0, 7: 1},
         compiler_params=limits,
         cost_estimate=cost(2_000_000_000),
         name="far",
-    )(listed, place, density, far, rest, store, out)[1]
+    )(listed, place, density, first, last, rest, store, out)[1]
 
 
 def solution(mesh):

time: 33.7 us -> 31.7 us (0.941)
  waiting for transfers between devices: 3.74 us -> 1.81 us
  Pallas kernels: 19 us -> 18.3 us
  between operations: 0.13 us -> 0.78 us
    ppermute x1, waiting for transfers between devices: 3.38 us -> 0.01 us  [local(): swapped = lax.ppermute(near, ('layer', 'grid'), swap_pairs)]
    ppermute x2, starting transfers between devices: 0.21 us -> 1.98 us  [the longest x1 1.89 us: local(): first = lax.ppermute(first, 'grid', outer_pairs)]
    ppermute x1, waiting for transfers between devices: 0.01 us -> 1.76 us  [local(): near = lax.ppermute(picked, 'grid', outer_pairs)]
    ppermute x1, starting transfers between devices: 8.15 us -> 6.45 us  [local(): near = lax.ppermute(picked, 'grid', outer_pairs)]
    pallas_call x5 -> x4, Pallas kernels: 13.4 us -> 12.4 us  [the longest x1 6.79 us: local(): pl.pallas_call(close_kernel, out_shape=(store_shape, shape(ROWS, BS, SPAN...]
    pallas_call x1, Pallas kernels: 2.66 us -> 3.21 us  [local(): pl.pallas_call(far_kernel, out_shape=(store_shape, out_shape), in_specs=[...]
  transfers between devices with their start and end apart: 4 -> 4, of which waited for: 2 -> 1; matrix products, arithmetic and copies ran while one was open for 2% -> 3% of each run, Pallas kernels for 43% -> 42%
where the time goes in v4:
time: 31.7 us; the launch traced here: 31.6 us
  Pallas kernels  18.3 us (58%)
  starting transfers between devices  9.71 us (31%)
  waiting for transfers between devices  1.81 us (6%)
  between operations  0.78 us (2%)
  local copies, waits for them, and re-layouts  0.64 us (2%)
    pallas_call x1, Pallas kernels, local(): pl.pallas_call(close_kernel, out_shape=(store_shape, shape(ROWS, BS, SPAN...  6.79 us
    ppermute x1, starting transfers between devices, local(): near = lax.ppermute(picked, 'grid', outer_pairs)  6.45 us
    pallas_call x1, Pallas kernels, local(): pl.pallas_call(far_kernel, out_shape=(store_shape, out_shape), in_specs=[...  3.21 us
    pallas_call x1, Pallas kernels, local(): pl.pallas_call(swapped_kernel, out_shape=(store_shape, shape(FAR, BS, SPA...  2.78 us
    pallas_call x1, Pallas kernels, local(): pl.pallas_call(early_pack_kernel, out_shape=(shape(FIRST, BS, BS), shape(...  2.42 us
    ppermute x1, starting transfers between devices, local(): first = lax.ppermute(first, 'grid', outer_pairs)  1.89 us
    pallas_call x1, Pallas kernels, local(): pl.pallas_call(pick_kernel, out_shape=(shape(BS, SHARE * BS), jax.ShapeDt...  1.85 us
    ppermute x1, waiting for transfers between devices, local(): near = lax.ppermute(picked, 'grid', outer_pairs)  1.76 us
  transfers between devices with their start and end apart: 4, of which 1 were waited for; matrix products, arithmetic and copies ran while one was open for 3% of the time, Pallas kernels for 42%

profile of v4, /device:TPU:16, one launch (start us, length us, event | category | flops | bytes accessed | tf_op | source)
XLA Modules:
  0.0 31.6 jit_solution(216393050063320446)
XLA Ops:
  0.0 0.0 copy-start.2
  0.0 0.0 copy-start.3
  0.0 1.8 %pick.1 = (bf16[128,1536]{1,0:T(8,128)(2,1)S(1)}, s32[8,128]{1,0:T(8,128)S(1)}, s32[1]{0:T(128)}) custom-call(bf16[8,128,1024]{2,1,0:T(8,128)(2,1)} %own.5, s32[8,512]{1,0:T(8,128)} %bitcast.34), custom_call_target="tpu_custom_call" | custom-call | tf_op jit(solution)/shard_map/pick/pallas_call | solution.py:375
  1.9 0.1 collective-permute-start.4
  2.0 2.4 %early_pack.1 = (bf16[28,128,128]{2,1,0:T(8,128)(2,1)S(1)}, bf16[12,128,128]{2,1,0:T(8,128)(2,1)S(1)}) custom-call(s32[8,128]{1,0:T(8,128)S(1)} %get-tuple-element.35.moves, bf16[8,128,1024]{2,1,0:T(8,128)(2,1)} %own.5), custom_call_target="tpu_custom_call" | custom-call | tf_op jit(solution)/shard_map/early_pack/pallas_call | solution.py:398
  4.4 6.4 %collective-permute-start.2 = (bf16[128,1536]{1,0:T(8,128)(2,1)S(1)}, bf16[128,1536]{1,0:T(8,128)(2,1)S(1)}, u32[]{:S(2)}, u32[]{:S(2)}) collective-permute-start(bf16[128,1536]{1,0:T(8,128)(2,1)S(1)} %get-tuple-element.45), channel_id=1, source_target_pairs={{0,63},{1,2},{2,1},{3,4},{4,3},{5,6},{6,5},{7,8},{8,7},{9,10},{10,... | collective-permute-start | bytes 1179656 | tf_op jit(solution)/shard_map/ppermute | solution.py:407
  10.8 1.3 %late_pack.1 = (bf16[28,128,128]{2,1,0:T(8,128)(2,1)S(1)}, s32[40]{0:T(128)S(1)}) custom-call(s32[8,128]{1,0:T(8,128)S(1)} %get-tuple-element.35.moves, bf16[8,128,1024]{2,1,0:T(8,128)(2,1)} %own.5, bf16[28,128,128]{2,1,0:T(8,128)(2,1)S(1)} %get-tuple-element.41._), custom_call_target="tpu_custom_call", output_to_operand_aliasing={{0}: (2, {})} | custom-call | tf_op jit(solution)/shard_map/late_pack/pallas_call | solution.py:408
  12.2 1.9 %collective-permute-start.1 = (bf16[28,128,128]{2,1,0:T(8,128)(2,1)S(1)}, bf16[28,128,128]{2,1,0:T(8,128)(2,1)S(1)}, u32[]{:S(2)}, u32[]{:S(2)}) collective-permute-start(bf16[28,128,128]{2,1,0:T(8,128)(2,1)S(1)} %get-tuple-element.43), channel_id=1, source_target_pairs={{0,63},{1,2},{2,1},{3,4},{4,3},{5,6},{6,5},{7,8},{8,7},{9,10},{10,... | collective-permute-start | bytes 2752520 | tf_op jit(solution)/shard_map/ppermute | solution.py:417
  14.0 0.0 copy-done.1
  14.0 0.1 fusion.11
  14.1 0.1 compare_select_fusion
  14.2 0.1 rev.3
  14.3 0.1 reshape.48
  14.4 0.1 copy.12
  14.4 0.0 copy-done.2
  14.4 0.0 copy-done.3
  14.5 0.1 pad_add_fusion
  14.5 1.8 %collective-permute-done.2.near = bf16[128,1536]{1,0:T(8,128)(2,1)S(1)} collective-permute-done((bf16[128,1536]{1,0:T(8,128)(2,1)S(1)}, bf16[128,1536]{1,0:T(8,128)(2,1)S(1)}, u32[]{:S(2)}, u32[]{:S(2)}) %collective-permute-start.2) | collective-permute-done | bytes 393248 | tf_op jit(solution)/shard_map/ppermute | solution.py:407
  16.3 1.3 %collective-permute-start.3 = (bf16[128,1536]{1,0:T(8,128)(2,1)S(1)}, bf16[128,1536]{1,0:T(8,128)(2,1)S(1)}, u32[]{:S(2)}, u32[]{:S(2)}) collective-permute-start(bf16[128,1536]{1,0:T(8,128)(2,1)S(1)} %collective-permute-done.2.near), channel_id=1, source_target_pairs={{0,64},{1,193},{2,66},{3,195},{4,68},{5,197},{6,70},{7,199},{8,72}... | collective-permute-start | bytes 1179656 | tf_op jit(solution)/shard_map/ppermute | solution.py:446
  17.6 0.1 select_select_fusion
  17.7 0.1 slice.59
  17.8 0.1 copy.11
  17.9 0.1 reshape.47.listed
  18.6 0.1 reshape.54.place
  18.7 0.0 copy-start
  18.7 0.0 collective-permute-done.4.inner
  18.7 6.8 %close.1 = (bf16[193,128,128]{2,1,0:T(8,128)(2,1)S(1)}, f32[8,128,1024]{2,1,0:T(8,128)S(1)}) custom-call(s32[64]{0:T(128)S(1)} %reshape.47.listed, s32[600]{0:T(1024)S(1)} %reshape.54.place, bf16[8,128,1024]{2,1,0:T(8,128)(2,1)} %own.5, bf16[8,128,1024]{2,1,0:T(8,128)(2,1)} %collective-permute-done.4.inner, bf16[128,1536]{1,0:T(8,128)(2,1)S(1)} %collective-permute-done.2.near), custom_call_target="tpu_custom_call" | custom-call | flops 4000000000 | bytes 4000000 | tf_op jit(solution)/shard_map/close/pallas_call | solution.py:447
  25.5 0.0 collective-permute-done.3.swapped
  25.5 0.0 copy-done
  25.6 2.8 %swapped.1 = (bf16[193,128,128]{2,1,0:T(8,128)(2,1)S(1)}, f32[5,128,1024]{2,1,0:T(8,128)S(1)}, f32[8,128,256]{2,1,0:T(8,128)}) custom-call(s32[64]{0:T(128)S(1)} %reshape.47.listed, s32[600]{0:T(1024)S(1)} %reshape.54.place, bf16[8,128,1024]{2,1,0:T(8,128)(2,1)S(1)} %copy-done, ...), custom_call_target="tpu_custom_call", output_to_operand_aliasing={{0}: (5, {})} | custom-call | flops 2000000000 | bytes 4000000 | tf_op jit(solution)/shard_map/swapped/pallas_call | solution.py:456
  28.3 0.0 collective-permute-done.1.first
  28.4 3.2 %far.1 = (bf16[193,128,128]{2,1,0:T(8,128)(2,1)S(1)}, f32[8,128,256]{2,1,0:T(8,128)}) custom-call(s32[64]{0:T(128)S(1)} %reshape.47.listed, s32[600]{0:T(1024)S(1)} %reshape.54.place, bf16[8,128,1024]{2,1,0:T(8,128)(2,1)S(1)} %copy-done, bf16[28,128,128]{2,1,0:T(8,128)(2,1)S(1)} %collective-permute-done.1.first, ...), custom_call_target="tpu_custom_call", output_to_operand_aliasing={{0}: (6, {}), {1}: (7, {})} | custom-call | flops 2000000000 | bytes 4000000 | tf_op jit(solution)/shard_map/far/pallas_call | solution.py:467
  (5 shorter events, 0.0 us)
Async XLA Ops:
  0.0 14.4 %copy-start.2 = (s32[20,8]{0,1:T(8,128)S(1)}, s32[20,8]{0,1:T(8,128)}, u32[]{:S(2)}) copy-start(s32[20,8]{0,1:T(8,128)} %constant.43.clone) | copy-start | bytes 1924
  0.0 14.4 %copy-start.3 = (s32[20,8]{0,1:T(8,128)S(1)}, s32[20,8]{0,1:T(8,128)}, u32[]{:S(2)}) copy-start(s32[20,8]{0,1:T(8,128)} %constant.42.clone) | copy-start | bytes 1924
  0.0 14.0 %copy-start.1 = (s32[512,8]{0,1:T(8,128)S(1)}, s32[512,8]{0,1:T(8,128)}, u32[]{:S(2)}) copy-start(s32[512,8]{0,1:T(8,128)} %param.7) | copy-start | bytes 49156
  1.9 16.9 %collective-permute-start.4 = (bf16[8,128,1024]{2,1,0:T(8,128)(2,1)}, bf16[8,128,1024]{2,1,0:T(8,128)(2,1)}, u32[]{:S(2)}, u32[]{:S(2)}) collective-permute-start(bf16[8,128,1024]{2,1,0:T(8,128)(2,1)} %own.5), channel_id=1, source_target_pairs={{0,1},{1,0},{2,3},{3,2},{4,5},{5,4},{6,7},{7,6},{8,9},{9,8},{10,11... | collective-permute-start | bytes 6291464 | tf_op jit(solution)/shard_map/ppermute | solution.py:389
  4.4 11.9 %collective-permute-start.2 = (bf16[128,1536]{1,0:T(8,128)(2,1)S(1)}, bf16[128,1536]{1,0:T(8,128)(2,1)S(1)}, u32[]{:S(2)}, u32[]{:S(2)}) collective-permute-start(bf16[128,1536]{1,0:T(8,128)(2,1)S(1)} %get-tuple-element.45), channel_id=1, source_target_pairs={{0,63},{1,2},{2,1},{3,4},{4,3},{5,6},{6,5},{7,8},{8,7},{9,10},{10,... | collective-permute-start | bytes 1179656 | tf_op jit(solution)/shard_map/ppermute | solution.py:407
  12.2 16.2 %collective-permute-start.1 = (bf16[28,128,128]{2,1,0:T(8,128)(2,1)S(1)}, bf16[28,128,128]{2,1,0:T(8,128)(2,1)S(1)}, u32[]{:S(2)}, u32[]{:S(2)}) collective-permute-start(bf16[28,128,128]{2,1,0:T(8,128)(2,1)S(1)} %get-tuple-element.43), channel_id=1, source_target_pairs={{0,63},{1,2},{2,1},{3,4},{4,3},{5,6},{6,5},{7,8},{8,7},{9,10},{10,... | collective-permute-start | bytes 2752520 | tf_op jit(solution)/shard_map/ppermute | solution.py:417
  16.3 9.2 %collective-permute-start.3 = (bf16[128,1536]{1,0:T(8,128)(2,1)S(1)}, bf16[128,1536]{1,0:T(8,128)(2,1)S(1)}, u32[]{:S(2)}, u32[]{:S(2)}) collective-permute-start(bf16[128,1536]{1,0:T(8,128)(2,1)S(1)} %collective-permute-done.2.near), channel_id=1, source_target_pairs={{0,64},{1,193},{2,66},{3,195},{4,68},{5,197},{6,70},{7,199},{8,72}... | collective-permute-start | bytes 1179656 | tf_op jit(solution)/shard_map/ppermute | solution.py:446
  18.7 6.8 %copy-start = (bf16[8,128,1024]{2,1,0:T(8,128)(2,1)S(1)}, bf16[8,128,1024]{2,1,0:T(8,128)(2,1)}, u32[]{:S(2)}) copy-start(bf16[8,128,1024]{2,1,0:T(8,128)(2,1)} %own.5) | copy-start | bytes 6291460

commit v5 on v4

--- a/solution.py
+++ b/solution.py
@@ -45,7 +45,7 @@
     return np.array(rows, np.int32)
 
 
-def tables(pattern, far_places):
+def tables(pattern, moves):
     blocks = pattern.shape[0]
     g = lax.axis_index("grid")
     odd = g % 2 == 1
@@ -58,7 +58,9 @@
     listed = columns[ROWS : 2 * ROWS]
     columns = jnp.concatenate([columns, jnp.full((1, LISTED), -1, jnp.int32)], axis=0)
     at = jnp.where(odd, places(True), places(False))
-    at = jnp.concatenate([far_places.reshape(FAR, LISTED), at], axis=0)
+    far = jnp.where(odd, moves[:, WINDOW - FAR : WINDOW][:, ::-1], moves[:, :FAR]).T
+    far = jnp.where(far == FAR_BLOCKS, ZERO, FAR_AT + far)
+    at = jnp.concatenate([far, at], axis=0)
     xs = lax.broadcasted_iota(jnp.int32, (WINDOW + 1, WINDOW), 1)
     place = jnp.full((WINDOW + 1, WINDOW), ZERO, jnp.int32)
     for s in range(LISTED):
@@ -126,25 +128,18 @@
     return jnp.where(parity() == 1, w, ROWS - 1 - w)
 
 
-def pick_kernel(source, pattern, out, moves, flag, listed, sems):
+def pick_kernel(source, out, sems):
     whole = sent_row(FAR + 2 * half())
     start = pl.multiple_of(half() * (SPAN // 2), SPAN // 2)
     copies = [
-        pltpu.make_async_copy(pattern, listed, sems.at[0]),
-        pltpu.make_async_copy(source.at[whole], out.at[:, pl.ds(0, SPAN)], sems.at[1]),
+        pltpu.make_async_copy(source.at[whole], out.at[:, pl.ds(0, SPAN)], sems.at[0]),
         pltpu.make_async_copy(
-            source.at[sent_row(FAR + 1), :, pl.ds(start, SPAN // 2)], out.at[:, pl.ds(SPAN, SPAN // 2)], sems.at[2]
+            source.at[sent_row(FAR + 1), :, pl.ds(start, SPAN // 2)], out.at[:, pl.ds(SPAN, SPAN // 2)], sems.at[1]
         ),
     ]
     for copy in copies:
         copy.start()
-    copies[0].wait()
-    position, most = positions(listed[...])
-    blocks = pattern.shape[1]
-    shift = blocks - ROWS * lax.rem(lax.axis_index("grid") + lax.axis_size("grid") - 1, lax.axis_size("grid"))
-    moves[...] = pltpu.roll(position, lax.rem(shift, blocks), 1)[:, :BS]
-    flag[0] = (most > FIRST).astype(jnp.int32)
-    for copy in copies[1:]:
+    for copy in copies:
         copy.wait()
 
 
@@ -152,47 +147,49 @@
     return lax.rem(lax.axis_index("grid"), EARLY_EVERY) == 0
 
 
-def pack(moves, source, own, packed, sems):
+def pack(first, count, pattern, source, out, moves, listed, own, window, places, packed, sems):
+    fetch = pltpu.make_async_copy(pattern, listed, sems.at[0])
+    fetch.start()
     start = jnp.where(parity() == 1, 0, ROWS - FAR)
     rows = pltpu.make_async_copy(source.at[pl.ds(start, FAR)], own, sems.at[1])
     rows.start()
+    fetch.wait()
+    position, most = positions(listed[...])
+    blocks, grid = pattern.shape[1], lax.axis_size("grid")
+    shift = blocks - ROWS * lax.rem(lax.axis_index("grid") + grid - 1, grid)
+    position = pltpu.roll(position, lax.rem(shift, blocks), 1)[:, :BS]
+    lane = lax.broadcasted_iota(jnp.int32, position.shape, 1)
+    window[...] = jnp.where(lane == BS - 1, (most > FIRST).astype(jnp.int32), position)
+    scalars = pltpu.make_async_copy(window, places, sems.at[0])
+    scalars.start()
+    table = pltpu.make_async_copy(window, moves, sems.at[2])
+    table.start()
+    scalars.wait()
     rows.wait()
     for k in range(FAR):
         held = jnp.where(parity() == 1, k, FAR - 1 - k)
         for s in range(LISTED):
-            packed[moves[s, ROWS + sent_row(k)]] = own[held, :, s * BS : (s + 1) * BS]
-
-
-def pack_first(moves, source, first, own, packed, sems):
-    pack(moves, source, own, packed, sems)
-    copy = pltpu.make_async_copy(packed.at[pl.ds(0, FIRST)], first, sems.at[0])
+            packed[places[s, ROWS + sent_row(k)]] = own[held, :, s * BS : (s + 1) * BS]
+    copy = pltpu.make_async_copy(packed.at[pl.ds(first, count)], out, sems.at[0])
     copy.start()
     copy.wait()
-
-
-def early_pack_kernel(moves, source, first, unused, *scratch):
+    table.wait()
+
+
+def early_pack_kernel(pattern, source, first, moves, unused, *scratch):
     @pl.when(waits_long())
     def _():
-        pack_first(moves, source, first, *scratch)
-
-
-def late_pack_kernel(moves, source, _, first, far_places, *scratch):
-    for k in range(FAR):
-        row = jnp.where(parity() == 0, k, WINDOW - 1 - k)
-        for s in range(LISTED):
-            place = moves[s, row]
-            far_places[k * LISTED + s] = jnp.where(place == FAR_BLOCKS, ZERO, FAR_AT + place)
-
+        pack(0, FIRST, pattern, source, first, moves, *scratch)
+
+
+def late_pack_kernel(pattern, source, _f, _m, first, moves, *scratch):
     @pl.when(jnp.logical_not(waits_long()))
     def _():
-        pack_first(moves, source, first, *scratch)
-
-
-def pack_rest_kernel(moves, source, rest, own, packed, sems):
-    pack(moves, source, own, packed, sems)
-    copy = pltpu.make_async_copy(packed.at[pl.ds(FIRST, REST)], rest, sems.at[0])
-    copy.start()
-    copy.wait()
+        pack(0, FIRST, pattern, source, first, moves, *scratch)
+
+
+def pack_rest_kernel(*refs):
+    pack(FIRST, REST, *refs)
 
 
 class Blocks:
@@ -372,65 +369,66 @@
 
     in_hbm = pltpu.with_memory_space_constraint(density, pltpu.HBM)
     by_slot = pltpu.with_memory_space_constraint(pattern.T, pltpu.HBM)
-    picked, moves, flag = pl.pallas_call(
+    picked = pl.pallas_call(
         pick_kernel,
-        out_shape=(
-            shape(BS, SHARE * BS),
-            jax.ShapeDtypeStruct((LISTED, BS), jnp.int32),
-            jax.ShapeDtypeStruct((1,), jnp.int32),
-        ),
-        in_specs=[HBM, HBM],
-        out_specs=(VMEM, VMEM, SMEM),
-        scratch_shapes=[pltpu.VMEM(by_slot.shape, jnp.int32), pltpu.SemaphoreType.DMA((3,))],
+        out_shape=shape(BS, SHARE * BS),
+        in_specs=[HBM],
+        out_specs=VMEM,
+        scratch_shapes=[pltpu.SemaphoreType.DMA((2,))],
         compiler_params=small,
         name="pick",
-    )(in_hbm, by_slot)
+    )(in_hbm)
     inner_sent, picked = lax.optimization_barrier((density, picked))
     inner = lax.ppermute(inner_sent, "grid", inner_pairs)
     packing = dict(
         scratch_shapes=[
+            pltpu.VMEM(by_slot.shape, jnp.int32),
             pltpu.VMEM((FAR, BS, SPAN), jnp.bfloat16),
+            pltpu.VMEM((LISTED, BS), jnp.int32),
+            pltpu.SMEM((LISTED, BS), jnp.int32),
             pltpu.VMEM((FAR_BLOCKS + 1, BS, BS), jnp.bfloat16),
-            pltpu.SemaphoreType.DMA((2,)),
+            pltpu.SemaphoreType.DMA((3,)),
         ],
         compiler_params=small,
     )
-    first, unused = pl.pallas_call(
+    first_shape, rest_shape = shape(FIRST, BS, BS), shape(REST, BS, BS)
+    moves_shape = jax.ShapeDtypeStruct((LISTED, BS), jnp.int32)
+    first, moves, unused = pl.pallas_call(
         early_pack_kernel,
-        out_shape=(shape(FIRST, BS, BS), shape(REST, BS, BS)),
-        in_specs=[SMEM, HBM],
-        out_specs=(ANY, ANY),
+        out_shape=(first_shape, moves_shape, rest_shape),
+        in_specs=[HBM, HBM],
+        out_specs=(ANY, ANY, ANY),
         name="early_pack",
         **packing,
-    )(moves, in_hbm)
+    )(by_slot, in_hbm)
     picked, first = lax.optimization_barrier((picked, first))
     near = lax.ppermute(picked, "grid", outer_pairs)
-    first, far_places = pl.pallas_call(
+    first, moves = pl.pallas_call(
         late_pack_kernel,
-        out_shape=(shape(FIRST, BS, BS), jax.ShapeDtypeStruct((FAR_BLOCKS,), jnp.int32)),
-        in_specs=[SMEM, HBM, ANY],
-        out_specs=(ANY, SMEM),
-        input_output_aliases={2: 0},
+        out_shape=(first_shape, moves_shape),
+        in_specs=[HBM, HBM, ANY, ANY],
+        out_specs=(ANY, ANY),
+        input_output_aliases={2: 0, 3: 1},
         name="late_pack",
         **packing,
-    )(moves, in_hbm, first)
+    )(by_slot, in_hbm, first, moves)
     first = lax.ppermute(first, "grid", outer_pairs)
 
     def send_rest(_):
         rest = pl.pallas_call(
             pack_rest_kernel,
-            out_shape=shape(REST, BS, BS),
-            in_specs=[SMEM, HBM],
-            out_specs=ANY,
+            out_shape=(rest_shape, moves_shape),
+            in_specs=[HBM, HBM],
+            out_specs=(ANY, ANY),
             name="pack_rest",
             **packing,
-        )(moves, in_hbm)
+        )(by_slot, in_hbm)[0]
         return lax.ppermute(rest, "grid", outer_pairs)
 
-    last = lax.cond(flag[0] > 0, send_rest, lambda blocks: blocks, unused)
-
-    listed, place = tables(pattern, far_places)
-    listed, last = lax.optimization_barrier((listed, last))
+    last = lax.cond(moves[0, BS - 1] > 0, send_rest, lambda blocks: blocks, unused)
+
+    listed, place = tables(pattern, moves)
+    near, listed, place, last = lax.optimization_barrier((near, listed, place, last))
     store_shape = shape(STORE, BS, BS)
     out_shape = shape(ROWS, BS, 2 * BS, dtype=jnp.float32)
 

time: 31.7 us -> 29.2 us (0.921)
  Pallas kernels: 18.3 us -> 16.3 us
  waiting for transfers between devices: 1.81 us -> 0.85 us
  local copies, waits for them, and re-layouts: 0.64 us -> 1.2 us
    pallas_call x3, Pallas kernels: 5.57 us -> 3.41 us  [the longest x1 2.35 us: local(): pl.pallas_call(early_pack_kernel, out_shape=(first_shape, moves_shape, re...]
    ppermute x1, waiting for transfers between devices: 1.76 us -> 0.78 us  [local(): near = lax.ppermute(picked, 'grid', outer_pairs)]
    slice x0 -> x2, local copies, waits for them, and re-layouts: none -> 0.65 us  [the longest x1 0.58 us: local(): moves[0, BS - 1] > 0]
    ppermute x1, starting transfers between devices: 1.89 us -> 2.42 us  [local(): first = lax.ppermute(first, 'grid', outer_pairs)]
    ppermute x1, starting transfers between devices: 6.45 us -> 5.91 us  [local(): near = lax.ppermute(picked, 'grid', outer_pairs)]
  transfers between devices with their start and end apart: 4 -> 4, of which waited for: 1 -> 2; matrix products, arithmetic and copies ran while one was open for 3% -> 5% of each run, Pallas kernels for 42% -> 40%
where the time goes in v5:
time: 29.2 us; the launch traced here: 29.1 us
  Pallas kernels  16.3 us (56%)
  starting transfers between devices  9.71 us (33%)
  local copies, waits for them, and re-layouts  1.2 us (4%)
  waiting for transfers between devices  0.85 us (3%)
  between operations  0.77 us (3%)
  other arithmetic  0.31 us (1%)
    pallas_call x1, Pallas kernels, local(): pl.pallas_call(close_kernel, out_shape=(store_shape, shape(ROWS, BS, SPAN...  6.64 us
    ppermute x1, starting transfers between devices, local(): near = lax.ppermute(picked, 'grid', outer_pairs)  5.91 us
    pallas_call x1, Pallas kernels, local(): pl.pallas_call(far_kernel, out_shape=(store_shape, out_shape), in_specs=[...  3.43 us
    pallas_call x1, Pallas kernels, local(): pl.pallas_call(swapped_kernel, out_shape=(store_shape, shape(FAR, BS, SPA...  2.77 us
    ppermute x1, starting transfers between devices, local(): first = lax.ppermute(first, 'grid', outer_pairs)  2.42 us
    pallas_call x1, Pallas kernels, local(): pl.pallas_call(early_pack_kernel, out_shape=(first_shape, moves_shape, re...  2.35 us
    ppermute x1, starting transfers between devices, local(): swapped = lax.ppermute(near, ('layer', 'grid'), swap_pairs)  1.28 us
    pallas_call x1, Pallas kernels, local(): pl.pallas_call(pick_kernel, out_shape=shape(BS, SHARE * BS), in_specs=[HB...  1.04 us
  transfers between devices with their start and end apart: 4, of which 2 were waited for; matrix products, arithmetic and copies ran while one was open for 5% of the time, Pallas kernels for 40%

profile of v5, /device:TPU:16, one launch (start us, length us, event | category | flops | bytes accessed | tf_op | source)
XLA Modules:
  0.0 29.1 jit_solution(9854543380458637725)
XLA Ops:
  0.0 0.0 copy-start.3
  0.0 0.0 copy-start.4
  0.0 1.0 %pick.1 = bf16[128,1536]{1,0:T(8,128)(2,1)S(1)} custom-call(bf16[8,128,1024]{2,1,0:T(8,128)(2,1)} %own.5), custom_call_target="tpu_custom_call" | custom-call | tf_op jit(solution)/shard_map/pick/pallas_call | solution.py:372
  1.1 0.1 collective-permute-start.4
  1.2 2.4 %early_pack.1 = (bf16[28,128,128]{2,1,0:T(8,128)(2,1)S(1)}, s32[8,128]{1,0:T(8,128)S(1)}, bf16[12,128,128]{2,1,0:T(8,128)(2,1)S(1)}) custom-call(s32[8,512]{1,0:T(8,128)} %bitcast.36, bf16[8,128,1024]{2,1,0:T(8,128)(2,1)} %own.5), custom_call_target="tpu_custom_call" | custom-call | tf_op jit(solution)/shard_map/early_pack/pallas_call | solution.py:396
  3.5 5.9 %collective-permute-start.1 = (bf16[128,1536]{1,0:T(8,128)(2,1)S(1)}, bf16[128,1536]{1,0:T(8,128)(2,1)S(1)}, u32[]{:S(2)}, u32[]{:S(2)}) collective-permute-start(bf16[128,1536]{1,0:T(8,128)(2,1)S(1)} %pick.1), channel_id=1, source_target_pairs={{0,63},{1,2},{2,1},{3,4},{4,3},{5,6},{6,5},{7,8},{8,7},{9,10},{10,... | collective-permute-start | bytes 1179656 | tf_op jit(solution)/shard_map/ppermute | solution.py:405
  9.5 2.4 %collective-permute-start.2 = (bf16[28,128,128]{2,1,0:T(8,128)(2,1)S(1)}, bf16[28,128,128]{2,1,0:T(8,128)(2,1)S(1)}, u32[]{:S(2)}, u32[]{:S(2)}) collective-permute-start(bf16[28,128,128]{2,1,0:T(8,128)(2,1)S(1)} %get-tuple-element.44), channel_id=1, source_target_pairs={{0,63},{1,2},{2,1},{3,4},{4,3},{5,6},{6,5},{7,8},{8,7},{9,10},{10,... | collective-permute-start | bytes 2752520 | tf_op jit(solution)/shard_map/ppermute | solution.py:415
  11.9 0.0 copy-done.1
  11.9 0.1 fusion.11
  12.0 0.1 compare_select_fusion
  12.0 0.1 rev.6
  12.1 0.1 slice.70
  12.2 0.1 rev.7
  12.3 0.0 copy-done.3
  12.3 0.0 copy-done.4
  12.3 0.1 pad_add_fusion
  12.4 0.1 slice.68
  12.5 0.6 %slice.87 = s32[1,1]{1,0:T(1,128)} slice(s32[8,128]{1,0:T(8,128)S(1)} %get-tuple-element.40), slice={[0:1], [127:128]} | slice | bytes 8 | tf_op jit(solution)/shard_map/slice | solution.py:428
  13.0 0.1 copy.11
  13.1 0.1 reshape.44.listed
  13.9 0.1 select_select_fusion
  14.0 0.1 reshape.50.place
  14.1 0.0 copy-start
  14.1 0.8 %collective-permute-done.1.near = bf16[128,1536]{1,0:T(8,128)(2,1)S(1)} collective-permute-done((bf16[128,1536]{1,0:T(8,128)(2,1)S(1)}, bf16[128,1536]{1,0:T(8,128)(2,1)S(1)}, u32[]{:S(2)}, u32[]{:S(2)}) %collective-permute-start.1) | collective-permute-done | bytes 393248 | tf_op jit(solution)/shard_map/ppermute | solution.py:405
  14.9 1.3 %collective-permute-start.3 = (bf16[128,1536]{1,0:T(8,128)(2,1)S(1)}, bf16[128,1536]{1,0:T(8,128)(2,1)S(1)}, u32[]{:S(2)}, u32[]{:S(2)}) collective-permute-start(bf16[128,1536]{1,0:T(8,128)(2,1)S(1)} %collective-permute-done.1.near), channel_id=1, source_target_pairs={{0,64},{1,193},{2,66},{3,195},{4,68},{5,197},{6,70},{7,199},{8,72}... | collective-permute-start | bytes 1179656 | tf_op jit(solution)/shard_map/ppermute | solution.py:444
  16.2 0.0 collective-permute-done.4.inner
  16.2 6.6 %close.1 = (bf16[193,128,128]{2,1,0:T(8,128)(2,1)S(1)}, f32[8,128,1024]{2,1,0:T(8,128)S(1)}) custom-call(s32[64]{0:T(128)S(1)} %reshape.44.listed, s32[600]{0:T(1024)S(1)} %reshape.50.place, bf16[8,128,1024]{2,1,0:T(8,128)(2,1)} %own.5, bf16[8,128,1024]{2,1,0:T(8,128)(2,1)} %collective-permute-done.4.inner, bf16[128,1536]{1,0:T(8,128)(2,1)S(1)} %collective-permute-done.1.near), custom_call_target="tpu_custom_call" | custom-call | flops 4000000000 | bytes 4000000 | tf_op jit(solution)/shard_map/close/pallas_call | solution.py:445
  22.8 0.0 collective-permute-done.3.swapped
  22.8 0.0 copy-done
  22.8 2.8 %swapped.1 = (bf16[193,128,128]{2,1,0:T(8,128)(2,1)S(1)}, f32[5,128,1024]{2,1,0:T(8,128)S(1)}, f32[8,128,256]{2,1,0:T(8,128)}) custom-call(s32[64]{0:T(128)S(1)} %reshape.44.listed, s32[600]{0:T(1024)S(1)} %reshape.50.place, bf16[8,128,1024]{2,1,0:T(8,128)(2,1)S(1)} %copy-done, ...), custom_call_target="tpu_custom_call", output_to_operand_aliasing={{0}: (5, {})} | custom-call | flops 2000000000 | bytes 4000000 | tf_op jit(solution)/shard_map/swapped/pallas_call | solution.py:454
  25.6 0.1 collective-permute-done.2.first
  25.7 3.4 %far.1 = (bf16[193,128,128]{2,1,0:T(8,128)(2,1)S(1)}, f32[8,128,256]{2,1,0:T(8,128)}) custom-call(s32[64]{0:T(128)S(1)} %reshape.44.listed, s32[600]{0:T(1024)S(1)} %reshape.50.place, bf16[8,128,1024]{2,1,0:T(8,128)(2,1)S(1)} %copy-done, bf16[28,128,128]{2,1,0:T(8,128)(2,1)S(1)} %collective-permute-done.2.first, ...), custom_call_target="tpu_custom_call", output_to_operand_aliasing={{0}: (6, {}), {1}: (7, {})} | custom-call | flops 2000000000 | bytes 4000000 | tf_op jit(solution)/shard_map/far/pallas_call | solution.py:465
  (7 shorter events, 0.1 us)
Async XLA Ops:
  0.0 12.3 %copy-start.3 = (s32[20,8]{0,1:T(8,128)S(1)}, s32[20,8]{0,1:T(8,128)}, u32[]{:S(2)}) copy-start(s32[20,8]{0,1:T(8,128)} %constant.48.clone) | copy-start | bytes 1924
  0.0 12.3 %copy-start.4 = (s32[20,8]{0,1:T(8,128)S(1)}, s32[20,8]{0,1:T(8,128)}, u32[]{:S(2)}) copy-start(s32[20,8]{0,1:T(8,128)} %constant.47.clone) | copy-start | bytes 1924
  0.0 11.9 %copy-start.1 = (s32[512,8]{0,1:T(8,128)S(1)}, s32[512,8]{0,1:T(8,128)}, u32[]{:S(2)}) copy-start(s32[512,8]{0,1:T(8,128)} %param.7) | copy-start | bytes 49156
  1.1 15.1 %collective-permute-start.4 = (bf16[8,128,1024]{2,1,0:T(8,128)(2,1)}, bf16[8,128,1024]{2,1,0:T(8,128)(2,1)}, u32[]{:S(2)}, u32[]{:S(2)}) collective-permute-start(bf16[8,128,1024]{2,1,0:T(8,128)(2,1)} %own.5), channel_id=1, source_target_pairs={{0,1},{1,0},{2,3},{3,2},{4,5},{5,4},{6,7},{7,6},{8,9},{9,8},{10,11... | collective-permute-start | bytes 6291464 | tf_op jit(solution)/shard_map/ppermute | solution.py:382
  3.5 11.4 %collective-permute-start.1 = (bf16[128,1536]{1,0:T(8,128)(2,1)S(1)}, bf16[128,1536]{1,0:T(8,128)(2,1)S(1)}, u32[]{:S(2)}, u32[]{:S(2)}) collective-permute-start(bf16[128,1536]{1,0:T(8,128)(2,1)S(1)} %pick.1), channel_id=1, source_target_pairs={{0,63},{1,2},{2,1},{3,4},{4,3},{5,6},{6,5},{7,8},{8,7},{9,10},{10,... | collective-permute-start | bytes 1179656 | tf_op jit(solution)/shard_map/ppermute | solution.py:405
  9.5 16.2 %collective-permute-start.2 = (bf16[28,128,128]{2,1,0:T(8,128)(2,1)S(1)}, bf16[28,128,128]{2,1,0:T(8,128)(2,1)S(1)}, u32[]{:S(2)}, u32[]{:S(2)}) collective-permute-start(bf16[28,128,128]{2,1,0:T(8,128)(2,1)S(1)} %get-tuple-element.44), channel_id=1, source_target_pairs={{0,63},{1,2},{2,1},{3,4},{4,3},{5,6},{6,5},{7,8},{8,7},{9,10},{10,... | collective-permute-start | bytes 2752520 | tf_op jit(solution)/shard_map/ppermute | solution.py:415
  14.1 8.7 %copy-start = (bf16[8,128,1024]{2,1,0:T(8,128)(2,1)S(1)}, bf16[8,128,1024]{2,1,0:T(8,128)(2,1)}, u32[]{:S(2)}) copy-start(bf16[8,128,1024]{2,1,0:T(8,128)(2,1)} %own.5) | copy-start | bytes 6291460
  14.9 7.9 %collective-permute-start.3 = (bf16[128,1536]{1,0:T(8,128)(2,1)S(1)}, bf16[128,1536]{1,0:T(8,128)(2,1)S(1)}, u32[]{:S(2)}, u32[]{:S(2)}) collective-permute-start(bf16[128,1536]{1,0:T(8,128)(2,1)S(1)} %collective-permute-done.1.near), channel_id=1, source_target_pairs={{0,64},{1,193},{2,66},{3,195},{4,68},{5,197},{6,70},{7,199},{8,72}... | collective-permute-start | bytes 1179656 | tf_op jit(solution)/shard_map/ppermute | solution.py:444

commit v6 on v5

--- a/solution.py
+++ b/solution.py
@@ -216,11 +216,23 @@
         return total
 
 
-def close_kernel(listed, place, own, inner, near, store, partial):
-    for n, source in enumerate((own, inner)):
+def close_kernel(listed, place, own_hbm, inner, near, last, store, partial, own, other, sems):
+    count = ROWS // 4
+    fetches = [
+        pltpu.make_async_copy(source.at[pl.ds(r, count)], held.at[pl.ds(r, count)], sems.at[n, r // count])
+        for n, (source, held) in enumerate(((own_hbm, own), (inner, other)))
+        for r in range(0, ROWS, count)
+    ]
+    fill = pltpu.make_async_copy(last, store.at[pl.ds(FAR_AT + FIRST, REST)], sems.at[2, 0])
+    for copy in fetches:
+        copy.start()
+    fill.start()
+    for n, held in enumerate((own, other)):
         for r in range(ROWS):
+            if r % count == 0:
+                fetches[n * (ROWS // count) + r // count].wait()
             for s in range(LISTED):
-                store[n * INNER_AT + s * ROWS + r] = source[r, :, s * BS : (s + 1) * BS]
+                store[n * INNER_AT + s * ROWS + r] = held[r, :, s * BS : (s + 1) * BS]
     place_share(near, store, True)
     store[ZERO] = jnp.zeros((BS, BS), jnp.bfloat16)
     whole = FAR + 2 * half()
@@ -239,7 +251,8 @@
             )
         return carry
 
-    lax.fori_loop(0, ROWS, one_row, 0)
+    lax.fori_loop(0, ROWS, one_row, 0, unroll=2)
+    fill.wait()
 
 
 def chosen(blocks, low, high, index, most):
@@ -337,9 +350,9 @@
 
 
 def far_kernel(
-    listed, place, own, first, last, rest, _s, _o, store, out, total, square, result, index, out_sems, sems
+    listed, place, own, first, rest, _s, _o, store, out, total, square, result, index, out_sems, sems
 ):
-    insert([(first, FAR_AT, FIRST), (last, FAR_AT + FIRST, REST)], store, sems)
+    insert([(first, FAR_AT, FIRST)], store, sems)
     source = lambda e: rest.at[e]
     rows = list(range(FAR))
     add_rows(listed, place, store, own, source, total, rows, 0, FAR, [6, 4, 4, 2, 2], index)
@@ -445,12 +458,17 @@
     store, sums = pl.pallas_call(
         close_kernel,
         out_shape=(store_shape, shape(ROWS, BS, SPAN, dtype=jnp.float32)),
-        in_specs=[SMEM, SMEM, VMEM, VMEM, VMEM],
+        in_specs=[SMEM, SMEM, HBM, ANY, VMEM, ANY],
         out_specs=(VMEM, VMEM),
+        scratch_shapes=[
+            pltpu.VMEM(density.shape, density.dtype),
+            pltpu.VMEM(density.shape, density.dtype),
+            pltpu.SemaphoreType.DMA((3, 4)),
+        ],
         compiler_params=limits,
         cost_estimate=cost(4_000_000_000),
         name="close",
-    )(listed, place, density, inner, near)
+    )(listed, place, in_hbm, inner, near, last)
     store, rest, out = pl.pallas_call(
         swapped_kernel,
         out_shape=(store_shape, shape(FAR, BS, SPAN, dtype=jnp.float32), out_shape),
@@ -465,14 +483,14 @@
     return pl.pallas_call(
         far_kernel,
         out_shape=(store_shape, out_shape),
-        in_specs=[SMEM, SMEM] + [VMEM] * 5 + [ANY],
+        in_specs=[SMEM, SMEM] + [VMEM] * 4 + [ANY],
         out_specs=(VMEM, ANY),
-        scratch_shapes=working(FAR) + [pltpu.SemaphoreType.DMA((2,))],
-        input_output_aliases={6: 0, 7: 1},
+        scratch_shapes=working(FAR) + [pltpu.SemaphoreType.DMA((1,))],
+        input_output_aliases={5: 0, 6: 1},
         compiler_params=limits,
         cost_estimate=cost(2_000_000_000),
         name="far",
-    )(listed, place, density, first, last, rest, store, out)[1]
+    )(listed, place, density, first, rest, store, out)[1]
 
 
 def solution(mesh):

time: 29.2 us -> 29 us (level)
  Pallas kernels: 16.3 us -> 15.3 us
  waiting for transfers between devices: 0.85 us -> 1.65 us
    pallas_call x1, Pallas kernels: 6.64 us -> 5.89 us  [local(): pl.pallas_call(close_kernel, out_shape=(store_shape, shape(ROWS, BS, SPAN...]
    ppermute x1, waiting for transfers between devices: 0.01 us -> 0.59 us  [local(): swapped = lax.ppermute(near, ('layer', 'grid'), swap_pairs)]
  transfers between devices with their start and end apart: 4 -> 4, of which waited for: 2 -> 3; matrix products, arithmetic and copies ran while one was open for 5% -> 5% of each run, Pallas kernels for 40% -> 38%
where the time goes in v6:
time: 29 us; the launch traced here: 28.9 us
  Pallas kernels  15.3 us (53%)
  starting transfers between devices  9.71 us (33%)
  waiting for transfers between devices  1.65 us (6%)
  local copies, waits for them, and re-layouts  1.2 us (4%)
  between operations  0.76 us (3%)
  other arithmetic  0.31 us (1%)
    ppermute x1, starting transfers between devices, local(): near = lax.ppermute(picked, 'grid', outer_pairs)  5.91 us
    pallas_call x1, Pallas kernels, local(): pl.pallas_call(close_kernel, out_shape=(store_shape, shape(ROWS, BS, SPAN...  5.89 us
    pallas_call x1, Pallas kernels, local(): pl.pallas_call(far_kernel, out_shape=(store_shape, out_shape), in_specs=[...  3.25 us
    pallas_call x1, Pallas kernels, local(): pl.pallas_call(swapped_kernel, out_shape=(store_shape, shape(FAR, BS, SPA...  2.73 us
    ppermute x1, starting transfers between devices, local(): first = lax.ppermute(first, 'grid', outer_pairs)  2.42 us
    pallas_call x1, Pallas kernels, local(): pl.pallas_call(early_pack_kernel, out_shape=(first_shape, moves_shape, re...  2.35 us
    ppermute x1, starting transfers between devices, local(): swapped = lax.ppermute(near, ('layer', 'grid'), swap_pairs)  1.28 us
    pallas_call x1, Pallas kernels, local(): pl.pallas_call(pick_kernel, out_shape=shape(BS, SHARE * BS), in_specs=[HB...  1.04 us
  transfers between devices with their start and end apart: 4, of which 3 were waited for; matrix products, arithmetic and copies ran while one was open for 5% of the time, Pallas kernels for 38%

profile of v6, /device:TPU:16, one launch (start us, length us, event | category | flops | bytes accessed | tf_op | source)
XLA Modules:
  0.0 28.9 jit_solution(6015961512420368158)
XLA Ops:
  0.0 0.0 copy-start.3
  0.0 0.0 copy-start.4
  0.0 1.0 %pick.1 = bf16[128,1536]{1,0:T(8,128)(2,1)S(1)} custom-call(bf16[8,128,1024]{2,1,0:T(8,128)(2,1)} %own.3), custom_call_target="tpu_custom_call" | custom-call | tf_op jit(solution)/shard_map/pick/pallas_call | solution.py:385
  1.1 0.1 collective-permute-start.4
  1.2 2.4 %early_pack.1 = (bf16[28,128,128]{2,1,0:T(8,128)(2,1)S(1)}, s32[8,128]{1,0:T(8,128)S(1)}, bf16[12,128,128]{2,1,0:T(8,128)(2,1)S(1)}) custom-call(s32[8,512]{1,0:T(8,128)} %bitcast.36, bf16[8,128,1024]{2,1,0:T(8,128)(2,1)} %own.3), custom_call_target="tpu_custom_call" | custom-call | tf_op jit(solution)/shard_map/early_pack/pallas_call | solution.py:409
  3.5 5.9 %collective-permute-start.1 = (bf16[128,1536]{1,0:T(8,128)(2,1)S(1)}, bf16[128,1536]{1,0:T(8,128)(2,1)S(1)}, u32[]{:S(2)}, u32[]{:S(2)}) collective-permute-start(bf16[128,1536]{1,0:T(8,128)(2,1)S(1)} %pick.1), channel_id=1, source_target_pairs={{0,63},{1,2},{2,1},{3,4},{4,3},{5,6},{6,5},{7,8},{8,7},{9,10},{10,... | collective-permute-start | bytes 1179656 | tf_op jit(solution)/shard_map/ppermute | solution.py:418
  9.5 2.4 %collective-permute-start.2 = (bf16[28,128,128]{2,1,0:T(8,128)(2,1)S(1)}, bf16[28,128,128]{2,1,0:T(8,128)(2,1)S(1)}, u32[]{:S(2)}, u32[]{:S(2)}) collective-permute-start(bf16[28,128,128]{2,1,0:T(8,128)(2,1)S(1)} %get-tuple-element.44), channel_id=1, source_target_pairs={{0,63},{1,2},{2,1},{3,4},{4,3},{5,6},{6,5},{7,8},{8,7},{9,10},{10,... | collective-permute-start | bytes 2752520 | tf_op jit(solution)/shard_map/ppermute | solution.py:428
  11.9 0.0 copy-done.1
  11.9 0.1 fusion.11
  12.0 0.1 compare_select_fusion
  12.0 0.1 rev.6
  12.1 0.1 slice.70
  12.2 0.1 rev.7
  12.3 0.0 copy-done.3
  12.3 0.0 copy-done.4
  12.3 0.1 pad_add_fusion
  12.4 0.1 slice.68
  12.5 0.6 %slice.87 = s32[1,1]{1,0:T(1,128)} slice(s32[8,128]{1,0:T(8,128)S(1)} %get-tuple-element.40), slice={[0:1], [127:128]} | slice | bytes 8 | tf_op jit(solution)/shard_map/slice | solution.py:441
  13.0 0.1 copy.11
  13.1 0.1 reshape.44.listed
  13.9 0.1 select_select_fusion
  14.0 0.1 reshape.50.place
  14.1 0.0 copy-start
  14.1 0.8 %collective-permute-done.1.near = bf16[128,1536]{1,0:T(8,128)(2,1)S(1)} collective-permute-done((bf16[128,1536]{1,0:T(8,128)(2,1)S(1)}, bf16[128,1536]{1,0:T(8,128)(2,1)S(1)}, u32[]{:S(2)}, u32[]{:S(2)}) %collective-permute-start.1) | collective-permute-done | bytes 393248 | tf_op jit(solution)/shard_map/ppermute | solution.py:418
  14.9 1.3 %collective-permute-start.3 = (bf16[128,1536]{1,0:T(8,128)(2,1)S(1)}, bf16[128,1536]{1,0:T(8,128)(2,1)S(1)}, u32[]{:S(2)}, u32[]{:S(2)}) collective-permute-start(bf16[128,1536]{1,0:T(8,128)(2,1)S(1)} %collective-permute-done.1.near), channel_id=1, source_target_pairs={{0,64},{1,193},{2,66},{3,195},{4,68},{5,197},{6,70},{7,199},{8,72}... | collective-permute-start | bytes 1179656 | tf_op jit(solution)/shard_map/ppermute | solution.py:457
  16.2 0.0 collective-permute-done.4.inner
  16.2 5.9 %close.1 = (bf16[193,128,128]{2,1,0:T(8,128)(2,1)S(1)}, f32[8,128,1024]{2,1,0:T(8,128)S(1)}) custom-call(s32[64]{0:T(128)S(1)} %reshape.44.listed, s32[600]{0:T(1024)S(1)} %reshape.50.place, bf16[8,128,1024]{2,1,0:T(8,128)(2,1)} %own.3, bf16[8,128,1024]{2,1,0:T(8,128)(2,1)} %collective-permute-done.4.inner, ...), custom_call_target="tpu_custom_call" | custom-call | flops 4000000000 | bytes 4000000 | tf_op jit(solution)/shard_map/close/pallas_call | solution.py:458
  22.1 0.6 %collective-permute-done.3.swapped = bf16[128,1536]{1,0:T(8,128)(2,1)S(1)} collective-permute-done((bf16[128,1536]{1,0:T(8,128)(2,1)S(1)}, bf16[128,1536]{1,0:T(8,128)(2,1)S(1)}, u32[]{:S(2)}, u32[]{:S(2)}) %collective-permute-start.3) | collective-permute-done | bytes 393248 | tf_op jit(solution)/shard_map/ppermute | solution.py:457
  22.7 0.0 copy-done
  22.7 2.7 %swapped.1 = (bf16[193,128,128]{2,1,0:T(8,128)(2,1)S(1)}, f32[5,128,1024]{2,1,0:T(8,128)S(1)}, f32[8,128,256]{2,1,0:T(8,128)}) custom-call(s32[64]{0:T(128)S(1)} %reshape.44.listed, s32[600]{0:T(1024)S(1)} %reshape.50.place, bf16[8,128,1024]{2,1,0:T(8,128)(2,1)S(1)} %copy-done, ...), custom_call_target="tpu_custom_call", output_to_operand_aliasing={{0}: (5, {})} | custom-call | flops 2000000000 | bytes 4000000 | tf_op jit(solution)/shard_map/swapped/pallas_call | solution.py:472
  25.4 0.3 collective-permute-done.2.first
  25.7 3.2 %far.1 = (bf16[193,128,128]{2,1,0:T(8,128)(2,1)S(1)}, f32[8,128,256]{2,1,0:T(8,128)}) custom-call(s32[64]{0:T(128)S(1)} %reshape.44.listed, s32[600]{0:T(1024)S(1)} %reshape.50.place, bf16[8,128,1024]{2,1,0:T(8,128)(2,1)S(1)} %copy-done, bf16[28,128,128]{2,1,0:T(8,128)(2,1)S(1)} %collective-permute-done.2.first, ...), custom_call_target="tpu_custom_call", output_to_operand_aliasing={{0}: (5, {}), {1}: (6, {})} | custom-call | flops 2000000000 | bytes 4000000 | tf_op jit(solution)/shard_map/far/pallas_call | solution.py:483
  (7 shorter events, 0.1 us)
Async XLA Ops:
  0.0 12.3 %copy-start.3 = (s32[20,8]{0,1:T(8,128)S(1)}, s32[20,8]{0,1:T(8,128)}, u32[]{:S(2)}) copy-start(s32[20,8]{0,1:T(8,128)} %constant.48.clone) | copy-start | bytes 1924
  0.0 12.3 %copy-start.4 = (s32[20,8]{0,1:T(8,128)S(1)}, s32[20,8]{0,1:T(8,128)}, u32[]{:S(2)}) copy-start(s32[20,8]{0,1:T(8,128)} %constant.47.clone) | copy-start | bytes 1924
  0.0 11.9 %copy-start.1 = (s32[512,8]{0,1:T(8,128)S(1)}, s32[512,8]{0,1:T(8,128)}, u32[]{:S(2)}) copy-start(s32[512,8]{0,1:T(8,128)} %param.7) | copy-start | bytes 49156
  1.1 15.1 %collective-permute-start.4 = (bf16[8,128,1024]{2,1,0:T(8,128)(2,1)}, bf16[8,128,1024]{2,1,0:T(8,128)(2,1)}, u32[]{:S(2)}, u32[]{:S(2)}) collective-permute-start(bf16[8,128,1024]{2,1,0:T(8,128)(2,1)} %own.3), channel_id=1, source_target_pairs={{0,1},{1,0},{2,3},{3,2},{4,5},{5,4},{6,7},{7,6},{8,9},{9,8},{10,11... | collective-permute-start | bytes 6291464 | tf_op jit(solution)/shard_map/ppermute | solution.py:395
  3.5 11.4 %collective-permute-start.1 = (bf16[128,1536]{1,0:T(8,128)(2,1)S(1)}, bf16[128,1536]{1,0:T(8,128)(2,1)S(1)}, u32[]{:S(2)}, u32[]{:S(2)}) collective-permute-start(bf16[128,1536]{1,0:T(8,128)(2,1)S(1)} %pick.1), channel_id=1, source_target_pairs={{0,63},{1,2},{2,1},{3,4},{4,3},{5,6},{6,5},{7,8},{8,7},{9,10},{10,... | collective-permute-start | bytes 1179656 | tf_op jit(solution)/shard_map/ppermute | solution.py:418
  9.5 16.2 %collective-permute-start.2 = (bf16[28,128,128]{2,1,0:T(8,128)(2,1)S(1)}, bf16[28,128,128]{2,1,0:T(8,128)(2,1)S(1)}, u32[]{:S(2)}, u32[]{:S(2)}) collective-permute-start(bf16[28,128,128]{2,1,0:T(8,128)(2,1)S(1)} %get-tuple-element.44), channel_id=1, source_target_pairs={{0,63},{1,2},{2,1},{3,4},{4,3},{5,6},{6,5},{7,8},{8,7},{9,10},{10,... | collective-permute-start | bytes 2752520 | tf_op jit(solution)/shard_map/ppermute | solution.py:428
  14.1 8.6 %copy-start = (bf16[8,128,1024]{2,1,0:T(8,128)(2,1)S(1)}, bf16[8,128,1024]{2,1,0:T(8,128)(2,1)}, u32[]{:S(2)}) copy-start(bf16[8,128,1024]{2,1,0:T(8,128)(2,1)} %own.3) | copy-start | bytes 6291460
  14.9 7.8 %collective-permute-start.3 = (bf16[128,1536]{1,0:T(8,128)(2,1)S(1)}, bf16[128,1536]{1,0:T(8,128)(2,1)S(1)}, u32[]{:S(2)}, u32[]{:S(2)}) collective-permute-start(bf16[128,1536]{1,0:T(8,128)(2,1)S(1)} %collective-permute-done.1.near), channel_id=1, source_target_pairs={{0,64},{1,193},{2,66},{3,195},{4,68},{5,197},{6,70},{7,199},{8,72}... | collective-permute-start | bytes 1179656 | tf_op jit(solution)/shard_map/ppermute | solution.py:457

commit v7 on v6

--- a/solution.py
+++ b/solution.py
@@ -15,7 +15,7 @@
 NEAR = ROWS - FAR
 SHARE = NEAR * LISTED // 2
 FAR_BLOCKS = FAR * LISTED
-FIRST = 28
+FIRST = 27
 REST = FAR_BLOCKS - FIRST
 EARLY_EVERY = 16
 INNER_AT = ROWS * LISTED

time: 29 us -> 28.7 us (0.990)
  transfers between devices with their start and end apart: 4 -> 4, of which waited for: 3 -> 2; matrix products, arithmetic and copies ran while one was open for 5% -> 5% of each run, Pallas kernels for 38% -> 38%
where the time goes in v7:
time: 28.7 us
  Pallas kernels  15.3 us (53%)
  starting transfers between devices  9.71 us (34%)
  waiting for transfers between devices  1.42 us (5%)
  local copies, waits for them, and re-layouts  1.2 us (4%)
  between operations  0.77 us (3%)
  other arithmetic  0.31 us (1%)
    ppermute x1, starting transfers between devices, local(): near = lax.ppermute(picked, 'grid', outer_pairs)  5.95 us
    pallas_call x1, Pallas kernels, local(): pl.pallas_call(close_kernel, out_shape=(store_shape, shape(ROWS, BS, SPAN...  5.89 us
    pallas_call x1, Pallas kernels, local(): pl.pallas_call(far_kernel, out_shape=(store_shape, out_shape), in_specs=[...  3.21 us
    pallas_call x1, Pallas kernels, local(): pl.pallas_call(swapped_kernel, out_shape=(store_shape, shape(FAR, BS, SPA...  2.79 us
    ppermute x1, starting transfers between devices, local(): first = lax.ppermute(first, 'grid', outer_pairs)  2.38 us
    pallas_call x1, Pallas kernels, local(): pl.pallas_call(early_pack_kernel, out_shape=(first_shape, moves_shape, re...  2.31 us
    ppermute x1, starting transfers between devices, local(): swapped = lax.ppermute(near, ('layer', 'grid'), swap_pairs)  1.28 us
    pallas_call x1, Pallas kernels, local(): pl.pallas_call(pick_kernel, out_shape=shape(BS, SHARE * BS), in_specs=[HB...  1.04 us
  transfers between devices with their start and end apart: 4, of which 2 were waited for; matrix products, arithmetic and copies ran while one was open for 5% of the time, Pallas kernels for 38%

profile of v7, /device:TPU:16, one launch (start us, length us, event | category | flops | bytes accessed | tf_op | source)
XLA Modules:
  0.0 28.7 jit_solution(10448941047556171801)
XLA Ops:
  0.0 0.0 copy-start.3
  0.0 0.0 copy-start.4
  0.0 1.0 %pick.1 = bf16[128,1536]{1,0:T(8,128)(2,1)S(1)} custom-call(bf16[8,128,1024]{2,1,0:T(8,128)(2,1)} %own.3), custom_call_target="tpu_custom_call" | custom-call | tf_op jit(solution)/shard_map/pick/pallas_call | solution.py:385
  1.1 0.1 collective-permute-start.4
  1.2 2.3 %early_pack.1 = (bf16[27,128,128]{2,1,0:T(8,128)(2,1)S(1)}, s32[8,128]{1,0:T(8,128)S(1)}, bf16[13,128,128]{2,1,0:T(8,128)(2,1)S(1)}) custom-call(s32[8,512]{1,0:T(8,128)} %bitcast.36, bf16[8,128,1024]{2,1,0:T(8,128)(2,1)} %own.3), custom_call_target="tpu_custom_call" | custom-call | tf_op jit(solution)/shard_map/early_pack/pallas_call | solution.py:409
  3.5 6.0 %collective-permute-start.1 = (bf16[128,1536]{1,0:T(8,128)(2,1)S(1)}, bf16[128,1536]{1,0:T(8,128)(2,1)S(1)}, u32[]{:S(2)}, u32[]{:S(2)}) collective-permute-start(bf16[128,1536]{1,0:T(8,128)(2,1)S(1)} %pick.1), channel_id=1, source_target_pairs={{0,63},{1,2},{2,1},{3,4},{4,3},{5,6},{6,5},{7,8},{8,7},{9,10},{10,... | collective-permute-start | bytes 1179656 | tf_op jit(solution)/shard_map/ppermute | solution.py:418
  9.5 2.4 %collective-permute-start.2 = (bf16[27,128,128]{2,1,0:T(8,128)(2,1)S(1)}, bf16[27,128,128]{2,1,0:T(8,128)(2,1)S(1)}, u32[]{:S(2)}, u32[]{:S(2)}) collective-permute-start(bf16[27,128,128]{2,1,0:T(8,128)(2,1)S(1)} %get-tuple-element.44), channel_id=1, source_target_pairs={{0,63},{1,2},{2,1},{3,4},{4,3},{5,6},{6,5},{7,8},{8,7},{9,10},{10,... | collective-permute-start | bytes 2654216 | tf_op jit(solution)/shard_map/ppermute | solution.py:428
  11.8 0.0 copy-done.1
  11.8 0.1 fusion.11
  11.9 0.1 compare_select_fusion
  12.0 0.1 rev.6
  12.1 0.1 slice.70
  12.2 0.1 rev.7
  12.2 0.0 copy-done.3
  12.2 0.0 copy-done.4
  12.3 0.1 pad_add_fusion
  12.3 0.1 slice.68
  12.4 0.6 %slice.87 = s32[1,1]{1,0:T(1,128)} slice(s32[8,128]{1,0:T(8,128)S(1)} %get-tuple-element.40), slice={[0:1], [127:128]} | slice | bytes 8 | tf_op jit(solution)/shard_map/slice | solution.py:441
  13.0 0.1 copy.11
  13.1 0.1 reshape.44.listed
  13.8 0.1 select_select_fusion
  14.0 0.1 reshape.50.place
  14.1 0.0 copy-start
  14.1 0.8 %collective-permute-done.1.near = bf16[128,1536]{1,0:T(8,128)(2,1)S(1)} collective-permute-done((bf16[128,1536]{1,0:T(8,128)(2,1)S(1)}, bf16[128,1536]{1,0:T(8,128)(2,1)S(1)}, u32[]{:S(2)}, u32[]{:S(2)}) %collective-permute-start.1) | collective-permute-done | bytes 393248 | tf_op jit(solution)/shard_map/ppermute | solution.py:418
  14.9 1.3 %collective-permute-start.3 = (bf16[128,1536]{1,0:T(8,128)(2,1)S(1)}, bf16[128,1536]{1,0:T(8,128)(2,1)S(1)}, u32[]{:S(2)}, u32[]{:S(2)}) collective-permute-start(bf16[128,1536]{1,0:T(8,128)(2,1)S(1)} %collective-permute-done.1.near), channel_id=1, source_target_pairs={{0,64},{1,193},{2,66},{3,195},{4,68},{5,197},{6,70},{7,199},{8,72}... | collective-permute-start | bytes 1179656 | tf_op jit(solution)/shard_map/ppermute | solution.py:457
  16.2 0.0 collective-permute-done.4.inner
  16.2 5.9 %close.1 = (bf16[193,128,128]{2,1,0:T(8,128)(2,1)S(1)}, f32[8,128,1024]{2,1,0:T(8,128)S(1)}) custom-call(s32[64]{0:T(128)S(1)} %reshape.44.listed, s32[600]{0:T(1024)S(1)} %reshape.50.place, bf16[8,128,1024]{2,1,0:T(8,128)(2,1)} %own.3, bf16[8,128,1024]{2,1,0:T(8,128)(2,1)} %collective-permute-done.4.inner, ...), custom_call_target="tpu_custom_call" | custom-call | flops 4000000000 | bytes 4000000 | tf_op jit(solution)/shard_map/close/pallas_call | solution.py:458
  22.1 0.6 %collective-permute-done.3.swapped = bf16[128,1536]{1,0:T(8,128)(2,1)S(1)} collective-permute-done((bf16[128,1536]{1,0:T(8,128)(2,1)S(1)}, bf16[128,1536]{1,0:T(8,128)(2,1)S(1)}, u32[]{:S(2)}, u32[]{:S(2)}) %collective-permute-start.3) | collective-permute-done | bytes 393248 | tf_op jit(solution)/shard_map/ppermute | solution.py:457
  22.7 0.0 copy-done
  22.7 2.8 %swapped.1 = (bf16[193,128,128]{2,1,0:T(8,128)(2,1)S(1)}, f32[5,128,1024]{2,1,0:T(8,128)S(1)}, f32[8,128,256]{2,1,0:T(8,128)}) custom-call(s32[64]{0:T(128)S(1)} %reshape.44.listed, s32[600]{0:T(1024)S(1)} %reshape.50.place, bf16[8,128,1024]{2,1,0:T(8,128)(2,1)S(1)} %copy-done, ...), custom_call_target="tpu_custom_call", output_to_operand_aliasing={{0}: (5, {})} | custom-call | flops 2000000000 | bytes 4000000 | tf_op jit(solution)/shard_map/swapped/pallas_call | solution.py:472
  25.5 0.0 collective-permute-done.2.first
  25.5 3.2 %far.1 = (bf16[193,128,128]{2,1,0:T(8,128)(2,1)S(1)}, f32[8,128,256]{2,1,0:T(8,128)}) custom-call(s32[64]{0:T(128)S(1)} %reshape.44.listed, s32[600]{0:T(1024)S(1)} %reshape.50.place, bf16[8,128,1024]{2,1,0:T(8,128)(2,1)S(1)} %copy-done, bf16[27,128,128]{2,1,0:T(8,128)(2,1)S(1)} %collective-permute-done.2.first, ...), custom_call_target="tpu_custom_call", output_to_operand_aliasing={{0}: (5, {}), {1}: (6, {})} | custom-call | flops 2000000000 | bytes 4000000 | tf_op jit(solution)/shard_map/far/pallas_call | solution.py:483
  (7 shorter events, 0.1 us)
Async XLA Ops:
  0.0 12.2 %copy-start.3 = (s32[20,8]{0,1:T(8,128)S(1)}, s32[20,8]{0,1:T(8,128)}, u32[]{:S(2)}) copy-start(s32[20,8]{0,1:T(8,128)} %constant.48.clone) | copy-start | bytes 1924
  0.0 12.2 %copy-start.4 = (s32[20,8]{0,1:T(8,128)S(1)}, s32[20,8]{0,1:T(8,128)}, u32[]{:S(2)}) copy-start(s32[20,8]{0,1:T(8,128)} %constant.47.clone) | copy-start | bytes 1924
  0.0 11.8 %copy-start.1 = (s32[512,8]{0,1:T(8,128)S(1)}, s32[512,8]{0,1:T(8,128)}, u32[]{:S(2)}) copy-start(s32[512,8]{0,1:T(8,128)} %param.7) | copy-start | bytes 49156
  1.1 15.1 %collective-permute-start.4 = (bf16[8,128,1024]{2,1,0:T(8,128)(2,1)}, bf16[8,128,1024]{2,1,0:T(8,128)(2,1)}, u32[]{:S(2)}, u32[]{:S(2)}) collective-permute-start(bf16[8,128,1024]{2,1,0:T(8,128)(2,1)} %own.3), channel_id=1, source_target_pairs={{0,1},{1,0},{2,3},{3,2},{4,5},{5,4},{6,7},{7,6},{8,9},{9,8},{10,11... | collective-permute-start | bytes 6291464 | tf_op jit(solution)/shard_map/ppermute | solution.py:395
  3.5 11.4 %collective-permute-start.1 = (bf16[128,1536]{1,0:T(8,128)(2,1)S(1)}, bf16[128,1536]{1,0:T(8,128)(2,1)S(1)}, u32[]{:S(2)}, u32[]{:S(2)}) collective-permute-start(bf16[128,1536]{1,0:T(8,128)(2,1)S(1)} %pick.1), channel_id=1, source_target_pairs={{0,63},{1,2},{2,1},{3,4},{4,3},{5,6},{6,5},{7,8},{8,7},{9,10},{10,... | collective-permute-start | bytes 1179656 | tf_op jit(solution)/shard_map/ppermute | solution.py:418
  9.5 16.0 %collective-permute-start.2 = (bf16[27,128,128]{2,1,0:T(8,128)(2,1)S(1)}, bf16[27,128,128]{2,1,0:T(8,128)(2,1)S(1)}, u32[]{:S(2)}, u32[]{:S(2)}) collective-permute-start(bf16[27,128,128]{2,1,0:T(8,128)(2,1)S(1)} %get-tuple-element.44), channel_id=1, source_target_pairs={{0,63},{1,2},{2,1},{3,4},{4,3},{5,6},{6,5},{7,8},{8,7},{9,10},{10,... | collective-permute-start | bytes 2654216 | tf_op jit(solution)/shard_map/ppermute | solution.py:428
  14.1 8.6 %copy-start = (bf16[8,128,1024]{2,1,0:T(8,128)(2,1)S(1)}, bf16[8,128,1024]{2,1,0:T(8,128)(2,1)}, u32[]{:S(2)}) copy-start(bf16[8,128,1024]{2,1,0:T(8,128)(2,1)} %own.3) | copy-start | bytes 6291460
  14.9 7.8 %collective-permute-start.3 = (bf16[128,1536]{1,0:T(8,128)(2,1)S(1)}, bf16[128,1536]{1,0:T(8,128)(2,1)S(1)}, u32[]{:S(2)}, u32[]{:S(2)}) collective-permute-start(bf16[128,1536]{1,0:T(8,128)(2,1)S(1)} %collective-permute-done.1.near), channel_id=1, source_target_pairs={{0,64},{1,193},{2,66},{3,195},{4,68},{5,197},{6,70},{7,199},{8,72}... | collective-permute-start | bytes 1179656 | tf_op jit(solution)/shard_map/ppermute | solution.py:457
